TPU v7x, 256 devices: a whole 4x4x8 slice. The times are simulated.
256 devices in a mesh: segment: 8 (over z), col: 32 (over y, x, core).
Axes of the slice: x: 4, y: 4, z: 8, core: 2. Of those that a mesh axis runs over, the one named last changes fastest.
Arguments:
- incoming: bfloat16 [8, 4096, 8192], P('segment', 'col'), may hold values from -6 to 6
- hidden: bfloat16 [8, 4096, 14336], P('segment', 'col'), may hold values from -6 to 6
- basis: float32 [8, 8192, 4096], P('segment', None, 'col'), may hold values from -0.0625 to 0.0625
- eigvals: float32 [8, 4096], P('segment', 'col'), may hold values from 0.01 to 1
- query_grads: bfloat16 [8, 128, 8192], P('segment', 'col'), may hold values from -0.0625 to 0.0625
- query_hidden: bfloat16 [8, 128, 14336], P('segment', 'col'), may hold values from -0.046875 to 0.046875
Outputs:
- section_grads: bfloat16 [8, 4096, 8192], P('segment', 'col')
- scores: float32 [64, 8], P('col')
All inputs are finite; a program needn't handle non-finite values.
Results may differ from a plain program's by a relative error of at most 0.02.
Values may be sent and summed in bfloat16 or wider, within the bound.
A program may use at most 128 MiB of HBM per device.

v0:
```python
import jax
import jax.numpy as jnp
from jax import lax
from jax.sharding import PartitionSpec as P

K = 4096
SEQLEN = 64
QUERIES = 8
QLEN = 16


damp_ratio = 0.1


def passed_along(block, axis, distance):
    devices = range(lax.axis_size(axis))
    route = [(i - distance, i) for i in devices if i - distance in devices]
    return lax.ppermute(block, axis, route)


def body(incoming, hidden, basis, eigvals, query_grads, query_hidden):
    own_term = incoming[0]
    carried = own_term
    section_count = lax.axis_size("segment")
    for chain_step in range(section_count - 1):
        above = passed_along(carried, "segment", -1)
        carried = (own_term.astype(jnp.float32) + above.astype(jnp.float32)).astype(jnp.bfloat16)
    eigen_vals = eigvals[0]
    eigen_total = lax.psum(jnp.sum(eigen_vals), "col")
    damping = damp_ratio * eigen_total / K
    query_rows = lax.all_gather(query_grads[0], "col", axis=0, tiled=True)
    basis_slab = basis[0]
    projected = lax.dot_general(
        basis_slab,
        query_rows.astype(jnp.float32),
        (((0,), (1,)), ((), ())),
        precision=lax.Precision.HIGHEST,
    )
    weighted = projected / (eigen_vals + damping)[:, None]
    own_rows = lax.psum_scatter(
        jnp.dot(basis_slab, weighted, precision=lax.Precision.HIGHEST).astype(jnp.bfloat16),
        "col",
        scatter_dimension=0,
        tiled=True,
    )
    precond = lax.all_gather(own_rows, "col", axis=0, tiled=True)
    grad_match = jnp.dot(carried, precond, preferred_element_type=jnp.float32)
    hidden_rows = hidden[0]
    hidden_match = lax.dot_general(
        hidden_rows,
        lax.all_gather(query_hidden[0], "col", axis=0, tiled=True),
        (((1,), (1,)), ((), ())),
        preferred_element_type=jnp.float32,
    )
    products = grad_match * hidden_match
    seq_count = products.shape[0] // SEQLEN
    seq_scores = products.reshape(seq_count, SEQLEN, QUERIES, QLEN).sum(axis=(1, 3)) / (
        SEQLEN * QLEN
    )
    scores = lax.psum(seq_scores, "segment")
    return (carried[None], scores)


def solution(mesh):
    in_specs = (
        P("segment", "col", None),
        P("segment", "col", None),
        P("segment", None, "col"),
        P("segment", "col"),
        P("segment", "col", None),
        P("segment", "col", None),
    )
    out_specs = (P("segment", "col", None), P("col", None))
    return jax.shard_map(body, mesh=mesh, in_specs=in_specs, out_specs=out_specs, check_vma=False)
```

profile of v0, /device:TPU:30, one launch (start us, length us, event | category | flops | bytes accessed | tf_op | source)
XLA Modules:
  0.0 433.2 jit_solution(8661444098275200479)
XLA Ops:
  7.2 0.0 all-gather.8.cloned.1.call-start
  7.2 0.0 copy-start.3
  7.2 0.0 copy-start
  7.2 1.4 collective-permute-start
  8.7 48.4 %collective-permute-done = bf16[128,8192]{1,0:T(8,128)(2,1)S(1)} collective-permute-done((bf16[128,8192]{1,0:T(8,128)(2,1)}, bf16[128,8192]{1,0:T(8,128)(2,1)S(1)}, u32[]{:S(2)}, u32[]{:S(2)}) %collective-permute-start) | collective-permute-done | bytes 2097184 | tf_op jit(solution)/shard_map/ppermute | solution.py:18
  57.0 3.4 fusion.1
  60.4 1.3 collective-permute-start.1
  61.7 0.0 copy-done.3
  61.7 0.8 copy.13
  62.5 0.0 all-gather.8.cloned.1.call-update
  62.5 0.0 copy-start.4
  62.5 0.0 reduce-scatter.2.cloned.1.call-start
  62.6 46.9 %collective-permute-done.1 = bf16[128,8192]{1,0:T(8,128)(2,1)} collective-permute-done((bf16[128,8192]{1,0:T(8,128)(2,1)}, bf16[128,8192]{1,0:T(8,128)(2,1)}, u32[]{:S(2)}, u32[]{:S(2)}) %collective-permute-start.1) | collective-permute-done | bytes 2097184 | tf_op jit(solution)/shard_map/ppermute | solution.py:18
  109.5 0.0 copy-done
  109.5 3.5 fusion.2
  113.0 1.3 collective-permute-start.2
  114.3 0.0 copy-done.4
  114.3 0.6 reduce_sum.18
  114.9 57.8 %psum.14 = f32[]{:T(128)} all-reduce(f32[]{:T(128)} %reduce_sum.18), channel_id=1, replica_groups=mesh['segment'=8,'col'=32] {'col'}, use_global_device_ids=true, to_apply=%region_1.0 | all-reduce | flops 1 | bytes 8 | tf_op jit(solution)/shard_map/psum | solution.py:29
  173.3 0.0 all-gather.8.cloned.1.call-done
  173.4 0.0 copy-start.1
  173.4 8.6 %fusion.17 = f32[128,128]{1,0:T(8,128)S(1)} fusion(bf16[1,128,8192]{2,0,1:T(2,128)(2,1)} %all-gather.8.cloned.1.call-done, f32[1,8192,128]{2,1,0:T(8,128)} %param.8, f32[128]{0:T(128)S(1)} %add_bitcast_fusion), kind=kOutput, calls=%fused_computation.26 | convolution fusion | flops 1610629120 | bytes 6357504 | tf_op jit(solution)/shard_map/dot_general | solution.py:33
  181.9 0.0 copy-done.1
  181.9 4.9 %fusion = bf16[8192,128]{0,1:T(8,128)(2,1)} fusion(f32[128,128]{1,0:T(8,128)S(1)} %fusion.17, f32[1,8192,128]{2,1,0:T(8,128)S(1)} %copy-done.1), kind=kOutput, calls=%fused_computation.8 | convolution fusion | flops 1611661312 | bytes 6356992 | tf_op jit(solution)/shard_map/dot_general | solution.py:41
  186.9 0.0 reduce-scatter.2.cloned.1.call-update
  186.9 0.0 copy-start.2
  186.9 0.0 all-gather.10.cloned.1.call-start
  186.9 0.0 collective-permute-done.2
  187.0 3.4 fusion.3
  190.4 1.3 collective-permute-start.3
  191.6 0.0 copy-done.2
  191.7 0.9 copy.14
  192.5 0.0 all-gather.10.cloned.1.call-update
  192.6 0.0 all-gather.6.cloned.1.call-start
  192.6 46.2 %collective-permute-done.3 = bf16[128,8192]{1,0:T(8,128)(2,1)} collective-permute-done((bf16[128,8192]{1,0:T(8,128)(2,1)}, bf16[128,8192]{1,0:T(8,128)(2,1)}, u32[]{:S(2)}, u32[]{:S(2)}) %collective-permute-start.3) | collective-permute-done | bytes 2097184 | tf_op jit(solution)/shard_map/ppermute | solution.py:18
  238.8 2.1 fusion.4
  240.9 1.3 collective-permute-start.4
  242.2 48.3 %collective-permute-done.4 = bf16[128,8192]{1,0:T(8,128)(2,1)S(1)} collective-permute-done((bf16[128,8192]{1,0:T(8,128)(2,1)S(1)}, bf16[128,8192]{1,0:T(8,128)(2,1)S(1)}, u32[]{:S(2)}, u32[]{:S(2)}) %collective-permute-start.4) | collective-permute-done | bytes 2097184 | tf_op jit(solution)/shard_map/ppermute | solution.py:18
  290.5 1.8 fusion.5
  292.3 1.5 collective-permute-start.5
  293.8 0.0 reduce-scatter.2.cloned.1.call-done
  293.8 0.0 all-gather.6.cloned.1.call-update
  293.8 48.7 %collective-permute-done.5 = bf16[128,8192]{1,0:T(8,128)(2,1)} collective-permute-done((bf16[128,8192]{1,0:T(8,128)(2,1)}, bf16[128,8192]{1,0:T(8,128)(2,1)}, u32[]{:S(2)}, u32[]{:S(2)}) %collective-permute-start.5) | collective-permute-done | bytes 2097184 | tf_op jit(solution)/shard_map/ppermute | solution.py:18
  342.6 3.4 fusion.6
  346.0 1.3 collective-permute-start.6
  347.2 0.0 all-gather.10.cloned.1.call-done
  347.3 6.7 %fusion.11 = f32[128,128]{1,0:T(8,128)S(1)} fusion(bf16[1,128,14336]{2,0,1:T(2,128)(2,1)} %all-gather.10.cloned.1.call-done, bf16[1,128,14336]{2,1,0:T(8,128)(2,1)} %param.7), kind=kOutput, calls=%fused_computation.19 | convolution fusion | flops 469762048 | bytes 7405568 | tf_op jit(solution)/shard_map/dot_general | solution.py:49
  354.0 35.5 %all-gather.6.cloned.1.call-done = bf16[8192,128]{0,1:T(8,128)(2,1)} async-done(((bf16[256,128]{0,1:T(8,128)(2,1)}), bf16[8192,128]{0,1:T(8,128)(2,1)}) %all-gather.6.cloned.1.call-update) | async-done | bytes 2097168 | tf_op jit(solution)/shard_map/all_gather | solution.py:46
  389.4 8.8 %collective-permute-done.6 = bf16[128,8192]{1,0:T(8,128)(2,1)} collective-permute-done((bf16[128,8192]{1,0:T(8,128)(2,1)}, bf16[128,8192]{1,0:T(8,128)(2,1)}, u32[]{:S(2)}, u32[]{:S(2)}) %collective-permute-start.6) | collective-permute-done | bytes 2097184 | tf_op jit(solution)/shard_map/ppermute | solution.py:18
  398.3 3.0 convolution_multiply_fusion
  401.3 0.1 copy.15
  401.4 0.1 reshape.14
  401.6 0.1 reduce_sum.19
  401.7 20.9 %psum.15 = f32[2,8]{0,1:T(8,128)S(1)} all-reduce(f32[2,8]{0,1:T(8,128)S(1)} %broadcast_multiply_fusion), channel_id=1, replica_groups=mesh['segment'=8,'col'=32] {'segment'}, use_global_device_ids=true, to_apply=%region_4.0 | all-reduce | flops 16 | bytes 128 | tf_op jit(solution)/shard_map/psum | solution.py:60
  422.6 0.6 copy.16
  423.2 3.4 fusion.23
  (2 shorter events, 0.0 us)
Async XLA Ops:
  7.2 166.2 %all-gather.8.cloned.1.call-start = ((), (), s32[]{:S(2)}) async-start(), calls=%async_computation.3 | async-start | bytes 4325376 | tf_op jit(solution)/shard_map/all_gather | solution.py:31
  7.2 54.5 %copy-start.3 = (bf16[1,4,8192]{2,1,0:T(4,128)(2,1)S(1)}, bf16[1,4,8192]{2,1,0:T(4,128)(2,1)}, u32[]{:S(2)}) copy-start(bf16[1,4,8192]{2,1,0:T(4,128)(2,1)} %param.10) | copy-start | bytes 196612
  7.2 102.3 %copy-start = (bf16[1,128,8192]{2,1,0:T(8,128)(2,1)S(1)}, bf16[1,128,8192]{2,1,0:T(8,128)(2,1)}, u32[]{:S(2)}) copy-start(bf16[1,128,8192]{2,1,0:T(8,128)(2,1)} %param.6) | copy-start | bytes 6291460
  7.2 49.8 %collective-permute-start = (bf16[128,8192]{1,0:T(8,128)(2,1)}, bf16[128,8192]{1,0:T(8,128)(2,1)S(1)}, u32[]{:S(2)}, u32[]{:S(2)}) collective-permute-start(bf16[128,8192]{1,0:T(8,128)(2,1)} %bitcast.40), channel_id=1, source_target_pairs={{32,0},{64,32},{96,64},{128,96},{160,128},{192,160},{224,192},{33,... | collective-permute-start | bytes 6291464 | tf_op jit(solution)/shard_map/ppermute | solution.py:18
  60.4 49.1 %collective-permute-start.1 = (bf16[128,8192]{1,0:T(8,128)(2,1)}, bf16[128,8192]{1,0:T(8,128)(2,1)}, u32[]{:S(2)}, u32[]{:S(2)}) collective-permute-start(bf16[128,8192]{1,0:T(8,128)(2,1)} %fusion.1), channel_id=1, source_target_pairs={{32,0},{64,32},{96,64},{128,96},{160,128},{192,160},{224,192},{33,... | collective-permute-start | bytes 6291464 | tf_op jit(solution)/shard_map/ppermute | solution.py:18
  62.5 51.8 %copy-start.4 = (f32[1,128]{1,0:T(1,128)S(1)}, f32[1,128]{1,0:T(1,128)}, u32[]{:S(2)}) copy-start(f32[1,128]{1,0:T(1,128)} %param.9) | copy-start | bytes 1540
  62.5 231.3 %reduce-scatter.2.cloned.1.call-start = ((), (), s32[]{:S(2)}) async-start(), calls=%async_computation.1 | async-start | bytes 2162688 | tf_op jit(solution)/shard_map/reduce_scatter | solution.py:40
  113.0 73.9 %collective-permute-start.2 = (bf16[128,8192]{1,0:T(8,128)(2,1)}, bf16[128,8192]{1,0:T(8,128)(2,1)}, u32[]{:S(2)}, u32[]{:S(2)}) collective-permute-start(bf16[128,8192]{1,0:T(8,128)(2,1)} %fusion.2), channel_id=1, source_target_pairs={{32,0},{64,32},{96,64},{128,96},{160,128},{192,160},{224,192},{33,... | collective-permute-start | bytes 6291464 | tf_op jit(solution)/shard_map/ppermute | solution.py:18
  173.4 8.6 %copy-start.1 = (f32[1,8192,128]{2,1,0:T(8,128)S(1)}, f32[1,8192,128]{2,1,0:T(8,128)}, u32[]{:S(2)}) copy-start(f32[1,8192,128]{2,1,0:T(8,128)} %param.8) | copy-start | bytes 12582916
  186.9 4.8 %copy-start.2 = (bf16[1,4,14336]{2,1,0:T(4,128)(2,1)S(1)}, bf16[1,4,14336]{2,1,0:T(4,128)(2,1)}, u32[]{:S(2)}) copy-start(bf16[1,4,14336]{2,1,0:T(4,128)(2,1)} %param.11) | copy-start | bytes 344068
  186.9 160.4 %all-gather.10.cloned.1.call-start = ((), (), s32[]{:S(2)}) async-start(), calls=%async_computation.4 | async-start | bytes 7569408 | tf_op jit(solution)/shard_map/all_gather | solution.py:51
  190.4 48.4 %collective-permute-start.3 = (bf16[128,8192]{1,0:T(8,128)(2,1)}, bf16[128,8192]{1,0:T(8,128)(2,1)}, u32[]{:S(2)}, u32[]{:S(2)}) collective-permute-start(bf16[128,8192]{1,0:T(8,128)(2,1)} %fusion.3), channel_id=1, source_target_pairs={{32,0},{64,32},{96,64},{128,96},{160,128},{192,160},{224,192},{33,... | collective-permute-start | bytes 6291464 | tf_op jit(solution)/shard_map/ppermute | solution.py:18
  192.6 196.9 %all-gather.6.cloned.1.call-start = ((), (), s32[]{:S(2)}) async-start(), calls=%async_computation.2 | async-start | bytes 2162688 | tf_op jit(solution)/shard_map/all_gather | solution.py:46
  240.9 49.6 %collective-permute-start.4 = (bf16[128,8192]{1,0:T(8,128)(2,1)S(1)}, bf16[128,8192]{1,0:T(8,128)(2,1)S(1)}, u32[]{:S(2)}, u32[]{:S(2)}) collective-permute-start(bf16[128,8192]{1,0:T(8,128)(2,1)S(1)} %fusion.4), channel_id=1, source_target_pairs={{32,0},{64,32},{96,64},{128,96},{160,128},{192,160},{224,192},{33,... | collective-permute-start | bytes 6291464 | tf_op jit(solution)/shard_map/ppermute | solution.py:18
  292.3 50.2 %collective-permute-start.5 = (bf16[128,8192]{1,0:T(8,128)(2,1)}, bf16[128,8192]{1,0:T(8,128)(2,1)}, u32[]{:S(2)}, u32[]{:S(2)}) collective-permute-start(bf16[128,8192]{1,0:T(8,128)(2,1)} %fusion.5), channel_id=1, source_target_pairs={{32,0},{64,32},{96,64},{128,96},{160,128},{192,160},{224,192},{33,... | collective-permute-start | bytes 6291464 | tf_op jit(solution)/shard_map/ppermute | solution.py:18
  346.0 52.3 %collective-permute-start.6 = (bf16[128,8192]{1,0:T(8,128)(2,1)}, bf16[128,8192]{1,0:T(8,128)(2,1)}, u32[]{:S(2)}, u32[]{:S(2)}) collective-permute-start(bf16[128,8192]{1,0:T(8,128)(2,1)} %fusion.6), channel_id=1, source_target_pairs={{32,0},{64,32},{96,64},{128,96},{160,128},{192,160},{224,192},{33,... | collective-permute-start | bytes 6291464 | tf_op jit(solution)/shard_map/ppermute | solution.py:18
Sparse Core Ops, SparseCore 0:
  62.6 53.4 all-gather.7
  187.0 93.0 reduce-scatter.1
  282.7 55.3 all-gather.9
  340.4 48.9 all-gather.5
where the time goes:
time: 434 us; the launch traced here: 433 us
  waiting for transfers between devices  283 us (65%)
  blocking collectives  78.6 us (18%)
  matrix products  23.2 us (5%)
  other arithmetic  21.8 us (5%)
  between operations  14.6 us (3%)
  starting transfers between devices  9.46 us (2%)
    ppermute x7, waiting for transfers between devices, passed_along(): return lax.ppermute(block, axis, route)  247 us
    psum x1, blocking collectives, body(): eigen_total = lax.psum(jnp.sum(eigen_vals), 'col')  57.8 us
    all_gather x1, waiting for transfers between devices, body(): precond = lax.all_gather(own_rows, 'col', axis=0, tiled=True)  35.5 us
    psum x1, blocking collectives, body(): scores = lax.psum(seq_scores, 'segment')  20.9 us
    convert_element_type x6, other arithmetic, body(): (own_term.astype(jnp.float32) + above.astype(jnp.float32)).astype(jnp.bfl...  17.6 us
    ppermute x7, starting transfers between devices, passed_along(): return lax.ppermute(block, axis, route)  9.3 us
  transfers between devices with their start and end apart: 11, of which 7 were waited for; matrix products, arithmetic and copies ran while one was open for 8% of the time, Pallas kernels for 0%

commit v1 on v0

v1 whole, which is shorter than its diff:
```python
import jax
import jax.numpy as jnp
from jax import lax
from jax.experimental import pallas as pl
from jax.experimental.pallas import tpu as pltpu
from jax.sharding import PartitionSpec as P

D = 8192
F = 14336
K = 4096
SEQLEN = 64
QLEN = 16
DAMP = 0.1

LAYERS = 8
W = 128
NCH = D // W
CHAIN = True
COL = True

f32 = jnp.float32
bf16 = jnp.bfloat16
MESH = pl.DeviceIdType.MESH


def remote(src, dst, ssem, rsem, dev):
    return pltpu.make_async_remote_copy(
        src_ref=src, dst_ref=dst, send_sem=ssem, recv_sem=rsem, device_id=dev, device_id_type=MESH
    )


def split(v):
    hi = v.astype(bf16)
    return hi, (v - hi.astype(f32)).astype(bf16)


def kernel(
    inc, hid, bas, eig, qg, qh,
    out, scores,
    own, rcv, hidv, basv,
    a1g, a1h, qgv, qhv, ebs, ebr,
    part_out, part_in, mine, r1s, r1r, r2s, r2r, prec,
    wmat, accp, gm, hm, share,
    ld_sem, chain_s, chain_r, out_sem, cs, cr, zs, zr,
):
    z = lax.axis_index("segment")
    col = lax.axis_index("col")
    c = lax.rem(col, 2)
    x = lax.rem(col // 2, 4)
    y = col // 8
    a1 = x + c * (y - x)
    a2 = y + c * (x - y)
    step1 = 2 + 6 * c
    step2 = 8 - 6 * c

    def on1(s):
        return (z, col + (lax.rem(a1 + s, 4) - a1) * step1)

    def on2(s):
        return (z, col + (lax.rem(a2 + s, 4) - a2) * step2)

    def onz(s):
        return (lax.rem(z + s, LAYERS), col)

    sibling = (z, col + 1 - 2 * c)
    below = (lax.rem(z + LAYERS - 1, LAYERS), col)

    def load_own(i, _):
        pltpu.make_async_copy(inc.at[0, :, pl.ds(pl.multiple_of(i * W, W), W)], own.at[i], ld_sem.at[0]).start()
        return 0

    lax.fori_loop(0, NCH, load_own, 0)
    load_bas = pltpu.make_async_copy(bas.at[0], basv, ld_sem.at[1])
    load_hid = pltpu.make_async_copy(hid.at[0], hidv, ld_sem.at[2])
    load_bas.start()
    load_hid.start()

    barrier = pltpu.get_barrier_semaphore()
    greeted = [sibling] + [on1(s) for s in (1, 2, 3)] + [on2(s) for s in (1, 2, 3)]
    greeted += [onz(s) for s in range(1, LAYERS)]
    for dev in greeted:
        pl.semaphore_signal(barrier, inc=1, device_id=dev, device_id_type=MESH)
    pl.semaphore_wait(barrier, len(greeted))

    sent = []
    counter = [0]

    def post(src, dst, dev):
        n = counter[0]
        counter[0] += 1
        copy = remote(src, dst, cs.at[n], cr.at[n], dev)
        sent.append(copy)
        copy.start()
        return copy

    def link(i):
        return remote(own.at[i], rcv.at[i], chain_s, chain_r.at[i], below)

    def store_out(i):
        pltpu.make_async_copy(own.at[i], out.at[0, :, pl.ds(pl.multiple_of(i * W, W), W)], out_sem).start()

    def chain_step(t):
        if not CHAIN:
            return
        i = t - 2 * (LAYERS - 1 - z)

        @pl.when(jnp.logical_and(jnp.logical_and(i >= 0, i < NCH), z < LAYERS - 1))
        def _():
            link(i).wait_recv()
            own[i] = (own[i].astype(f32) + rcv[i].astype(f32)).astype(bf16)

            @pl.when(z > 0)
            def _():
                link(i).start()

            store_out(i)

    now = [0]

    def slots(n, fn=None):
        base = now[0]

        def step(j, _):
            chain_step(base + j)
            if fn is not None:
                fn(j)
            return 0

        if not CHAIN and fn is None:
            now[0] += n
            return
        lax.fori_loop(0, n, step, 0)
        now[0] += n

    if COL:
        g1 = [post(qg, a1g.at[pl.ds(a1 * 16, 16)], on1(s)) for s in (1, 2, 3)]
        ebs[0] = jnp.broadcast_to(eig[...], (8, 128))
        e1 = [post(ebs.at[0], ebr.at[s - 1], on1(s)) for s in (1, 2, 3)]
        h1 = [post(qh, a1h.at[pl.ds(a1 * 16, 16)], on1(s)) for s in (1, 2, 3)]

    pltpu.make_async_copy(own, own, ld_sem.at[0]).wait()

    if CHAIN:
        @pl.when(z == LAYERS - 1)
        def _():
            def first(i, _):
                link(i).start()
                return 0

            lax.fori_loop(0, NCH, first, 0)

            def first_out(i, _):
                store_out(i)
                return 0

            lax.fori_loop(0, NCH, first_out, 0)

    def order16():
        r = lax.broadcasted_iota(jnp.int32, (64, 64), 0)
        k = lax.broadcasted_iota(jnp.int32, (64, 64), 1)
        src = ((r % 16) // 4) * 16 + (r % 4) * 4 + r // 16
        return (k == src).astype(f32).astype(bf16)

    def rows16(s):
        return pl.ds(pl.multiple_of(c * 64 + lax.rem(a2 + 4 - s, 4) * 16, 16), 16)

    def assemble(a, q, wide):
        part = jnp.dot(order16(), a[...], preferred_element_type=f32).astype(bf16)
        for s in range(4):
            q[rows16(0), s * wide:(s + 1) * wide] = part[s * 16:(s + 1) * 16]

    def gather2(q):
        second = [post(q.at[rows16(0)], q.at[rows16(0)], on2(s)) for s in (1, 2, 3)]
        swaps = [post(q.at[rows16(0)], q.at[rows16(0)], sibling)]
        return second, swaps

    if COL:
        a1g[pl.ds(pl.multiple_of(a1 * 16, 16), 16)] = qg[...]
        a1h[pl.ds(pl.multiple_of(a1 * 16, 16), 16)] = qh[...]
        slots(2)
        for copy in g1:
            copy.wait_recv()
        assemble(a1g, qgv, D // 4)
        g2, g3 = gather2(qgv)
        for copy in e1:
            copy.wait_recv()
        ebs[1] = ebs[0] + ebr[0] + ebr[1] + ebr[2]
        e2 = [post(ebs.at[1], ebr.at[2 + s], on2(s)) for s in (1, 2, 3)]
        slots(2)
        for copy in h1:
            copy.wait_recv()
        assemble(a1h, qhv, F // 4)
        for copy in e2:
            copy.wait_recv()
        ebs[2] = ebs[1] + ebr[3] + ebr[4] + ebr[5]
        e3 = post(ebs.at[2], ebr.at[6], sibling)
        for s in (1, 3, 2):
            slots(3)
            g2[s - 1].wait_recv()
            g3.append(post(qgv.at[rows16(s)], qgv.at[rows16(s)], sibling))
        h2, h3 = gather2(qhv)
        slots(2)
        load_bas.wait()
        for copy in g3:
            copy.wait_recv()
        e3.wait_recv()
        ebs[3] = ebs[2] + ebr[6]

        KB = 512
        accp[...] = jnp.zeros_like(accp)

        def project(j):
            at = pl.ds(pl.multiple_of(j * KB, KB), KB)
            hi, lo = split(basv[at])
            accp[...] += jnp.dot(qgv[:, at], jnp.concatenate([hi, lo], axis=1), preferred_element_type=f32)

        def project2(j):
            project(2 * j)
            project(2 * j + 1)

        slots(D // KB // 2, project2)
        damping = DAMP * jnp.sum(ebs[3][0:1], axis=1, keepdims=True) / K
        weighted = (accp[:, :128] + accp[:, 128:]) / (eig[...] + damping)
        hi, lo = split(weighted.T)
        wmat[0:128, 0:128] = hi
        wmat[128:256, 0:128] = hi
        wmat[0:128, 128:256] = lo
        wmat[128:256, 128:256] = jnp.zeros_like(lo)

        def expand(row):
            at = pl.ds(pl.multiple_of(row, KB), KB)
            hi, lo = split(basv[at])
            both = jnp.dot(jnp.concatenate([hi, lo], axis=1), wmat[...], preferred_element_type=f32)
            return both[:, :128] + both[:, 128:]

        pair = []
        for b in (1, 3, 2, 0):
            block = lax.rem(a2 + b, 4)

            def give(j, block=block):
                row = block * 1024 + j * KB
                part_out[pl.ds(pl.multiple_of(row, KB), KB)] = expand((1 - c) * 4096 + row).astype(bf16)

            slots(2, give)
            at = pl.ds(pl.multiple_of(block * 1024, 1024), 1024)
            pair.append(post(part_out.at[at], part_in.at[at], sibling))

        def keep(j):
            for half in (0, 1):
                row = (2 * j + half) * KB
                mine[pl.ds(pl.multiple_of(row, KB), KB)] = expand(c * 4096 + row)

        slots(4, keep)

        r1 = []
        for arrival, s in zip(pair, (1, 3, 2, 0)):
            block = lax.rem(a1 + s, 4)
            arrival.wait_recv()

            def add_pair(j, block=block):
                at = pl.ds(pl.multiple_of(block * 1024 + j * KB, KB), KB)
                total = mine[at] + part_in[at].astype(f32)
                mine[at] = total
                r1s[at] = total.astype(bf16)

            slots(2, add_pair)
            if s:
                at = pl.ds(pl.multiple_of(block * 1024, 1024), 1024)
                r1.append(post(r1s.at[at], r1r.at[s - 1], on1(s)))

        for s in (1, 3, 2):
            h2[s - 1].wait_recv()
            h3.append(post(qhv.at[rows16(s)], qhv.at[rows16(s)], sibling))
        slots(3)
        load_hid.wait()
        for copy in h3:
            copy.wait_recv()
        hm[...] = jnp.zeros_like(hm)

        def match_hidden(j):
            for half in range(4):
                at = pl.ds(pl.multiple_of((4 * j + half) * 512, 512), 512)
                hm[...] += lax.dot_general(
                    hidv[:, at], qhv[:, at], (((1,), (1,)), ((), ())), preferred_element_type=f32
                )

        slots(F // 2048, match_hidden)

        for copy in r1:
            copy.wait_recv()
        for s in (1, 3, 2, 0):
            sub = lax.rem(a2 + s, 4)
            at = pl.ds(pl.multiple_of(sub * 256, 256), 256)
            row = pl.ds(pl.multiple_of(a1 * 1024 + sub * 256, 256), 256)
            total = mine[row] + r1r[0, at].astype(f32) + r1r[1, at].astype(f32) + r1r[2, at].astype(f32)
            mine[row] = total
            r2s[at] = total.astype(bf16)
            if s == 1:
                r2 = []
            if s:
                r2.append(post(r2s.at[at], r2r.at[s - 1], on2(s)))
        slots(2)
        for copy in r2:
            copy.wait_recv()
        row = pl.ds(pl.multiple_of(a1 * 1024 + a2 * 256, 256), 256)
        total = mine[row] + r2r[0].astype(f32) + r2r[1].astype(f32) + r2r[2].astype(f32)
        own_rows = pl.ds(pl.multiple_of(c * 4096 + a1 * 1024 + a2 * 256, 256), 256)
        prec[own_rows] = total.astype(bf16)
        p1 = [post(prec.at[own_rows], prec.at[own_rows], on2(s)) for s in (1, 2, 3)]
        slots(2)
        for copy in p1:
            copy.wait_recv()

        def band(s):
            return pl.ds(pl.multiple_of(c * 4096 + lax.rem(a1 + 4 - s, 4) * 1024, 1024), 1024)

        p2 = [post(prec.at[band(0)], prec.at[band(0)], on1(s)) for s in (1, 2, 3)]
        p3 = [post(prec.at[band(0)], prec.at[band(0)], sibling)]
        for s in (1, 3, 2):
            slots(3)
            p2[s - 1].wait_recv()
            p3.append(post(prec.at[band(s)], prec.at[band(s)], sibling))
        slots(1)
        for copy in p3:
            copy.wait_recv()
    else:
        load_bas.wait()
        load_hid.wait()

    gm[...] = jnp.zeros_like(gm)
    total_slots = NCH + 2 * (LAYERS - 1)
    rest = total_slots - now[0]
    rest_needed = NCH // 4
    if rest > rest_needed:
        slots(rest - rest_needed)
        rest = rest_needed

    def match_one(i):
        gm[...] += jnp.dot(own[i], prec[pl.ds(pl.multiple_of(i * W, W), W)], preferred_element_type=f32)

    def match_grads(j):
        for k in range(4):
            match_one(4 * j + k)

    if COL:
        slots(rest_needed, match_grads)
    else:
        slots(rest_needed)

    if COL:
        prod = gm[...] * hm[...]
        pos = lax.broadcasted_iota(jnp.int32, (1, 128), 1)
        side = pos // 64
        p2nd = (pos // 16) % 4
        p1st = (pos // 4) % 4
        query = jnp.where(side == 0, p2nd * 2 + p1st // 2, p1st * 2 + p2nd // 2)
        sums = [jnp.sum(prod[s * SEQLEN:(s + 1) * SEQLEN], axis=0, keepdims=True) for s in (0, 1)]
        lane = lax.broadcasted_iota(jnp.int32, (8, 128), 1)
        line = lax.broadcasted_iota(jnp.int32, (8, 128), 0)
        tile = jnp.zeros((8, 128), f32)
        for s in (0, 1):
            for q in range(8):
                one = jnp.sum(jnp.where(query == q, sums[s], 0.0), axis=1, keepdims=True)
                tile = tile + jnp.where(jnp.logical_and(line == s, lane == q), one, 0.0)
        share[z] = tile / (SEQLEN * QLEN)
        zc = [remote(share.at[z], share.at[z], zs.at[s - 1], zr.at[s - 1], onz(s)) for s in range(1, LAYERS)]
        for copy in zc:
            copy.start()
        for copy in zc:
            copy.wait_recv()
        total = share[0]
        for s in range(1, LAYERS):
            total = total + share[s]
        scores[...] = total[0:2, 0:8]
        for copy in zc:
            copy.wait_send()
    for copy in sent:
        copy.wait_send()
    if CHAIN:
        @pl.when(z > 0)
        def _():
            remote(own, rcv, chain_s, chain_r.at[0], below).wait_send()

        pltpu.make_async_copy(own, own, out_sem).wait()


def column(incoming, hidden, basis, eigvals, query_grads, query_hidden):
    anyspace = pl.BlockSpec(memory_space=pl.ANY)
    vmem = pl.BlockSpec(memory_space=pltpu.VMEM)
    dma = pltpu.SemaphoreType.DMA
    section, scores = pl.pallas_call(
        kernel,
        out_shape=(
            jax.ShapeDtypeStruct((1, 128, D), bf16),
            jax.ShapeDtypeStruct((2, 8), f32),
        ),
        in_specs=[anyspace, anyspace, anyspace, vmem, vmem, vmem],
        out_specs=(anyspace, vmem),
        scratch_shapes=[
            pltpu.VMEM((NCH, 128, W), bf16),
            pltpu.VMEM((NCH, 128, W), bf16),
            pltpu.VMEM((128, F), bf16),
            pltpu.VMEM((D, 128), f32),
            pltpu.VMEM((64, D // 4), bf16),
            pltpu.VMEM((64, F // 4), bf16),
            pltpu.VMEM((128, D), bf16),
            pltpu.VMEM((128, F), bf16),
            pltpu.VMEM((4, 8, 128), f32),
            pltpu.VMEM((7, 8, 128), f32),
            pltpu.VMEM((4096, 128), bf16),
            pltpu.VMEM((4096, 128), bf16),
            pltpu.VMEM((4096, 128), f32),
            pltpu.VMEM((4096, 128), bf16),
            pltpu.VMEM((3, 1024, 128), bf16),
            pltpu.VMEM((1024, 128), bf16),
            pltpu.VMEM((3, 256, 128), bf16),
            pltpu.VMEM((D, 128), bf16),
            pltpu.VMEM((256, 256), bf16),
            pltpu.VMEM((128, 256), f32),
            pltpu.VMEM((128, 128), f32),
            pltpu.VMEM((128, 128), f32),
            pltpu.VMEM((LAYERS, 8, 128), f32),
            dma((3,)),
            dma,
            dma((NCH,)),
            dma,
            dma((48,)),
            dma((48,)),
            dma((LAYERS - 1,)),
            dma((LAYERS - 1,)),
        ],
        compiler_params=pltpu.CompilerParams(
            collective_id=0, has_side_effects=True, vmem_limit_bytes=56 * 1024 * 1024
        ),
    )(
        incoming,
        hidden,
        basis,
        eigvals,
        query_grads.reshape(16, D // 4),
        query_hidden.reshape(16, F // 4),
    )
    return section, scores


def solution(mesh):
    in_specs = (
        P("segment", "col", None),
        P("segment", "col", None),
        P("segment", None, "col"),
        P("segment", "col"),
        P("segment", "col", None),
        P("segment", "col", None),
    )
    out_specs = (P("segment", "col", None), P("col", None))
    return jax.shard_map(column, mesh=mesh, in_specs=in_specs, out_specs=out_specs, check_vma=False)
```

time: 434 us -> 113 us (0.26)
  the two profiles are of different devices: /device:TPU:30 before, /device:TPU:40 now
where the time goes in v1:
time: 113 us
  Pallas kernels  105 us (93%)
  local copies, waits for them, and re-layouts  6.79 us (6%)
    pallas_call x1, Pallas kernels, column(): pl.pallas_call(kernel, out_shape=(jax.ShapeDtypeStruct((1, 128, D), bf16)...  105 us
    unnamed x4, local copies, waits for them, and re-layouts  3.66 us

profile of v1, /device:TPU:40, one launch (start us, length us, event | category | flops | bytes accessed | tf_op | source)
XLA Modules:
  0.0 112.6 jit_solution(4707741864560378209)
XLA Ops:
  0.6 1.5 %reshape.10.qg = bf16[16,2048]{1,0:T(8,128)(2,1)} reshape(bf16[1,4,8192]{2,1,0:T(4,128)(2,1)} %param.10) | data formatting | bytes 131072 | tf_op jit(solution)/shard_map/reshape | solution.py:440
  2.1 1.6 %reshape.11.qh = bf16[16,3584]{1,0:T(8,128)(2,1)} reshape(bf16[1,4,14336]{2,1,0:T(4,128)(2,1)} %param.11) | data formatting | bytes 229376 | tf_op jit(solution)/shard_map/reshape | solution.py:441
  3.8 105.1 %shard_map.77 = (bf16[1,128,8192]{2,1,0:T(8,128)(2,1)}, f32[2,8]{1,0:T(2,128)}) custom-call(bf16[1,128,8192]{2,1,0:T(8,128)(2,1)} %inc.1, bf16[1,128,14336]{2,1,0:T(8,128)(2,1)} %hid.1, f32[1,8192,128]{2,1,0:T(8,128)} %bas.1, f32[1,128]{1,0:T(1,128)} %eig.1, bf16[16,2048]{1,0:T(8,128)(2,1)} %reshape.10.qg, bf16[16,3584]{1,0:T(8,128)(2,1)} %reshape.11.qh), custom_call_target="tpu_custom_call" | custom-call | tf_op jit(solution)/shard_map/pallas_call | solution.py:391
  108.9 0.0 copy-start
  108.9 3.1 %copy.10 = bf16[1,128,8192]{2,1,0:T(8,128)(2,1)} copy(bf16[1,128,8192]{2,1,0:T(8,128)(2,1)} %get-tuple-element.4) | data formatting | bytes 4194304
  112.0 0.0 copy-done
  112.0 0.6 copy.11
Async XLA Ops:
  108.9 3.1 %copy-start = (f32[2,8]{1,0:T(2,128)S(1)}, f32[2,8]{1,0:T(2,128)}, u32[]{:S(2)}) copy-start(f32[2,8]{1,0:T(2,128)} %get-tuple-element.5) | copy-start | bytes 196

commit v2 on v1

v2 whole, which is shorter than its diff:
```python
import jax
import jax.numpy as jnp
from jax import lax
from jax.experimental import pallas as pl
from jax.experimental.pallas import tpu as pltpu
from jax.sharding import PartitionSpec as P

D = 8192
F = 14336
K = 4096
SEQLEN = 64
QLEN = 16
DAMP = 0.1

LAYERS = 8
W = 128
NCH = D // W
NZ = 6
NUP = NZ * (LAYERS - 1)
T_G1, T_H1, T_G2, T_G3, T_H2, T_R1, T_R2, T_P1, T_P2 = 6, 9, 15, 20, 32, 42, 47, 53, 61
PER_P = 4
CHAIN = True
COL = True

f32 = jnp.float32
bf16 = jnp.bfloat16
MESH = pl.DeviceIdType.MESH


def remote(src, dst, ssem, rsem, dev):
    return pltpu.make_async_remote_copy(
        src_ref=src, dst_ref=dst, send_sem=ssem, recv_sem=rsem, device_id=dev, device_id_type=MESH
    )


def split(v):
    hi = v.astype(bf16)
    return hi, (v - hi.astype(f32)).astype(bf16)


def kernel(
    inc, hid, bas, eig, qg, qh,
    out, scores,
    own, down, rcv, ups, upr, hidv, basv,
    g16, h16, a1g, a1h, qgv, qhv, ebs, ebr,
    part_out, part_in, mine, r1s, r1r, r2s, r2r, prec,
    wmat, accp, gm, hm, share,
    ld_sem, chain_s, chain_r, up_s, up_r, cs, cr, zs, zr,
):
    z = lax.axis_index("segment")
    col = lax.axis_index("col")
    c = lax.rem(col, 2)
    x = lax.rem(col // 2, 4)
    y = col // 8
    a1 = x + c * (y - x)
    a2 = y + c * (x - y)
    step1 = 2 + 6 * c
    step2 = 8 - 6 * c
    depth = LAYERS - 1 - z

    def on1(s):
        return (z, col + (lax.rem(a1 + s, 4) - a1) * step1)

    def on2(s):
        return (z, col + (lax.rem(a2 + s, 4) - a2) * step2)

    def onz(s):
        return (lax.rem(z + s, LAYERS), col)

    sibling = (z, col + 1 - 2 * c)

    barrier = pltpu.get_barrier_semaphore()
    greeted = [sibling] + [on1(s) for s in (1, 2, 3)] + [on2(s) for s in (1, 2, 3)]
    greeted += [onz(s) for s in range(1, LAYERS)]
    for dev in greeted:
        pl.semaphore_signal(barrier, inc=1, device_id=dev, device_id_type=MESH)

    load_own = pltpu.make_async_copy(inc.at[0], own, ld_sem.at[0])
    load_bas = pltpu.make_async_copy(bas.at[0], basv, ld_sem.at[1])
    load_hid = pltpu.make_async_copy(hid.at[0], hidv, ld_sem.at[2])
    load_own.start()
    load_bas.start()
    load_hid.start()

    def fold(q, wide):
        rows = q[0].astype(f32)
        return jnp.concatenate([rows[:, s * wide:(s + 1) * wide] for s in range(4)], axis=0).astype(bf16)

    g16[...] = fold(qg, D // 4)
    h16[...] = fold(qh, F // 4)
    ebs[0] = jnp.broadcast_to(eig[...], (8, 128))
    pl.semaphore_wait(barrier, len(greeted))

    sent = []
    counter = [0]

    def post(src, dst, dev):
        n = counter[0]
        counter[0] += 1
        copy = remote(src, dst, cs.at[n], cr.at[n], dev)
        sent.append(copy)
        copy.start()
        return copy

    def link(i):
        return remote(down.at[i], rcv.at[i], chain_s, chain_r.at[i], onz(LAYERS - 1))

    def uplink(i):
        return remote(ups.at[i], upr.at[i], up_s, up_r.at[i], onz(1))

    def lanes(i):
        return pl.ds(pl.multiple_of(i * W, W), W)

    def add(p, q):
        return (p.astype(f32) + q.astype(f32)).astype(bf16)

    def chunk_at(t):
        return lax.rem(t + NCH - NZ * depth, NCH)

    def chain_step(t):
        i = chunk_at(t)
        fed = jnp.logical_and(z < LAYERS - 1, t >= NZ)

        @pl.when(fed)
        def _():
            link(i).wait_recv()
            down[i] = add(own[:, lanes(i)], rcv[i])

        @pl.when(jnp.logical_not(fed))
        def _():
            down[i] = own[:, lanes(i)]

        @pl.when(jnp.logical_and(z > 0, t < NCH - NZ))
        def _():
            link(i).start()

        partial = t < NZ * depth

        @pl.when(jnp.logical_not(partial))
        def _():
            out[0, :, lanes(i)] = down[i]

        @pl.when(jnp.logical_and(partial, t // NZ >= 4))
        def _():
            out[0, :, lanes(i)] = add(down[i], upr[i - (NCH - NUP)])

    def up_step(t):
        hop = t // NZ
        cut = lax.rem(z - hop + LAYERS, LAYERS)

        @pl.when(cut > 0)
        def _():
            n = (cut - 1) * NZ + t - hop * NZ
            i = NCH - NUP + n
            last = hop == LAYERS - 1

            @pl.when(hop > 0)
            def _():
                uplink(n).wait_recv()

            @pl.when(jnp.logical_and(z >= cut, hop > 0))
            def _():
                ups[n] = add(own[:, lanes(i)], upr[n])

            @pl.when(jnp.logical_and(z >= cut, hop == 0))
            def _():
                ups[n] = own[:, lanes(i)]

            @pl.when(jnp.logical_and(z < cut, jnp.logical_not(last)))
            def _():
                ups[n] = upr[n]

            @pl.when(jnp.logical_not(last))
            def _():
                uplink(n).start()

            @pl.when(jnp.logical_and(z < cut, cut - z <= 4))
            def _():
                out[0, :, lanes(i)] = add(down[i], upr[n])

    now = [0]

    def slots(n, fn=None):
        if not CHAIN:
            now[0] = max(now[0], min(now[0] + n, NCH))
            if fn is not None:
                def plain(j, _):
                    fn(j)
                    return 0

                lax.fori_loop(0, n, plain, 0)
            return
        done = 0
        while done < n:
            base = now[0]
            stop = n - done
            if base < NZ * LAYERS:
                stop = min(stop, NZ * LAYERS - base)
            elif base < NCH:
                stop = min(stop, NCH - base)
            elif fn is None:
                return

            def step(j, _, base=base, done=done):
                if base < NCH:
                    chain_step(base + j)
                if base < NZ * LAYERS:
                    up_step(base + j)
                if fn is not None:
                    fn(done + j)
                return 0

            lax.fori_loop(0, stop, step, 0)
            now[0] += stop
            done += stop

    def until(t):
        if now[0] < t:
            slots(t - now[0])

    if COL:
        g1 = [post(g16, a1g.at[pl.ds(a1 * 16, 16)], on1(s)) for s in (1, 2, 3)]
        e1 = [post(ebs.at[0], ebr.at[s - 1], on1(s)) for s in (1, 2, 3)]
        h1 = [post(h16, a1h.at[pl.ds(a1 * 16, 16)], on1(s)) for s in (1, 2, 3)]

    load_own.wait()

    def order16():
        r = lax.broadcasted_iota(jnp.int32, (64, 64), 0)
        k = lax.broadcasted_iota(jnp.int32, (64, 64), 1)
        src = ((r % 16) // 4) * 16 + (r // 16) * 4 + r % 4
        return (k == src).astype(f32).astype(bf16)

    def rows16(s):
        return pl.ds(pl.multiple_of(c * 64 + lax.rem(a2 + 4 - s, 4) * 16, 16), 16)

    def assemble(a, q, wide):
        part = jnp.dot(order16(), a[...], preferred_element_type=f32).astype(bf16)
        for s in range(4):
            q[rows16(0), s * wide:(s + 1) * wide] = part[s * 16:(s + 1) * 16]

    def gather2(q):
        second = [post(q.at[rows16(0)], q.at[rows16(0)], on2(s)) for s in (1, 2, 3)]
        swaps = [post(q.at[rows16(0)], q.at[rows16(0)], sibling)]
        return second, swaps

    if COL:
        a1g[pl.ds(pl.multiple_of(a1 * 16, 16), 16)] = g16[...]
        a1h[pl.ds(pl.multiple_of(a1 * 16, 16), 16)] = h16[...]
        until(T_G1)
        for copy in g1:
            copy.wait_recv()
        assemble(a1g, qgv, D // 4)
        g2, g3 = gather2(qgv)
        for copy in e1:
            copy.wait_recv()
        ebs[1] = ebs[0] + ebr[0] + ebr[1] + ebr[2]
        e2 = [post(ebs.at[1], ebr.at[2 + s], on2(s)) for s in (1, 2, 3)]
        until(T_H1)
        for copy in h1:
            copy.wait_recv()
        assemble(a1h, qhv, F // 4)
        for copy in e2:
            copy.wait_recv()
        ebs[2] = ebs[1] + ebr[3] + ebr[4] + ebr[5]
        e3 = post(ebs.at[2], ebr.at[6], sibling)
        until(T_G2)
        h2, h3 = gather2(qhv)
        for s, t in zip((1, 3, 2), (T_G2, T_G2 + 1, T_G2 + 2)):
            until(t)
            g2[s - 1].wait_recv()
            g3.append(post(qgv.at[rows16(s)], qgv.at[rows16(s)], sibling))
        until(T_G3)
        load_bas.wait()
        for copy in g3:
            copy.wait_recv()
        e3.wait_recv()
        ebs[3] = ebs[2] + ebr[6]

        KB = 512
        accp[...] = jnp.zeros_like(accp)

        def project(j):
            for k in range(PER_P):
                at = pl.ds(pl.multiple_of((PER_P * j + k) * KB, KB), KB)
                hi, lo = split(basv[at])
                accp[...] += jnp.dot(qgv[:, at], jnp.concatenate([hi, lo], axis=1), preferred_element_type=f32)

        slots(D // KB // PER_P, project)
        damping = DAMP * jnp.sum(ebs[3][0:1], axis=1, keepdims=True) / K
        weighted = (accp[:, :128] + accp[:, 128:]) / (eig[...] + damping)
        hi, lo = split(weighted.T)
        wmat[0:128, 0:128] = hi
        wmat[128:256, 0:128] = hi
        wmat[0:128, 128:256] = lo
        wmat[128:256, 128:256] = jnp.zeros_like(lo)

        def expand(row):
            at = pl.ds(pl.multiple_of(row, KB), KB)
            hi, lo = split(basv[at])
            both = jnp.dot(jnp.concatenate([hi, lo], axis=1), wmat[...], preferred_element_type=f32)
            return both[:, :128] + both[:, 128:]

        pair = []
        for b in (1, 3, 2, 0):
            block = lax.rem(a2 + b, 4)

            def give(j, block=block):
                for k in range(2):
                    row = block * 1024 + (2 * j + k) * KB
                    part_out[pl.ds(pl.multiple_of(row, KB), KB)] = expand((1 - c) * 4096 + row).astype(bf16)

            slots(1, give)
            at = pl.ds(pl.multiple_of(block * 1024, 1024), 1024)
            pair.append(post(part_out.at[at], part_in.at[at], sibling))

        r1 = []
        for arrival, s in zip(pair, (1, 3, 2, 0)):
            block = lax.rem(a1 + s, 4)

            def keep(j, block=block):
                for k in range(2):
                    row = block * 1024 + (2 * j + k) * KB
                    mine[pl.ds(pl.multiple_of(row, KB), KB)] = expand(c * 4096 + row)

            slots(1, keep)
            arrival.wait_recv()
            at = pl.ds(pl.multiple_of(block * 1024, 1024), 1024)
            total = mine[at] + part_in[at].astype(f32)
            if s:
                r1s[at] = total.astype(bf16)
                r1.append(post(r1s.at[at], r1r.at[s - 1], on1(s)))
            else:
                mine[at] = total

        until(T_H2)
        for s in (1, 3, 2):
            h2[s - 1].wait_recv()
            h3.append(post(qhv.at[rows16(s)], qhv.at[rows16(s)], sibling))
            slots(1)
        load_hid.wait()
        for copy in h3:
            copy.wait_recv()
        hm[...] = jnp.zeros_like(hm)

        def match_hidden(j):
            for half in range(4):
                at = pl.ds(pl.multiple_of((4 * j + half) * 512, 512), 512)
                hm[...] += lax.dot_general(
                    hidv[:, at], qhv[:, at], (((1,), (1,)), ((), ())), preferred_element_type=f32
                )

        slots(F // 2048, match_hidden)

        until(T_R1)
        for copy in r1:
            copy.wait_recv()
        r2 = []
        for s in (1, 3, 2, 0):
            sub = lax.rem(a2 + s, 4)
            at = pl.ds(pl.multiple_of(sub * 256, 256), 256)
            row = pl.ds(pl.multiple_of(a1 * 1024 + sub * 256, 256), 256)
            total = mine[row] + r1r[0, at].astype(f32) + r1r[1, at].astype(f32) + r1r[2, at].astype(f32)
            if s:
                r2s[at] = total.astype(bf16)
                r2.append(post(r2s.at[at], r2r.at[s - 1], on2(s)))
            else:
                mine[row] = total
        until(T_R2)
        for copy in r2:
            copy.wait_recv()
        row = pl.ds(pl.multiple_of(a1 * 1024 + a2 * 256, 256), 256)
        total = mine[row] + r2r[0].astype(f32) + r2r[1].astype(f32) + r2r[2].astype(f32)
        own_rows = pl.ds(pl.multiple_of(c * 4096 + a1 * 1024 + a2 * 256, 256), 256)
        prec[own_rows] = total.astype(bf16)
        p1 = [post(prec.at[own_rows], prec.at[own_rows], on2(s)) for s in (1, 2, 3)]
        until(T_P1)
        for copy in p1:
            copy.wait_recv()

        def band(s):
            return pl.ds(pl.multiple_of(c * 4096 + lax.rem(a1 + 4 - s, 4) * 1024, 1024), 1024)

        p2 = [post(prec.at[band(0)], prec.at[band(0)], on1(s)) for s in (1, 2, 3)]
        p3 = {0: post(prec.at[band(0)], prec.at[band(0)], sibling)}

        gm[...] = jnp.zeros_like(gm)

        def match_one(i):
            gm[...] += jnp.dot(
                out[0, :, lanes(i)], prec[pl.ds(pl.multiple_of(i * W, W), W)], preferred_element_type=f32
            )

        def first_chunk(mine_half, s):
            side, at = (c, a1) if mine_half else (1 - c, a2)
            return side * (NCH // 2) + lax.rem(at + 4 - s, 4) * 8

        def match_band(mine_half, s, wait=0):
            first = first_chunk(mine_half, s)
            seen = now[0]

            def pair_of(j):
                for k in (0, 1):
                    i = first + 2 * j + k
                    if seen >= NCH or not CHAIN:
                        match_one(i)
                    else:
                        @pl.when(lax.rem(i + NZ * depth, NCH) < seen)
                        def _(i=i):
                            match_one(i)

            slots(4, pair_of)
            return seen

        began = {}
        began[True, 0] = match_band(True, 0)
        p3[0].wait_recv()
        began[False, 0] = match_band(False, 0)
        until(T_P2)
        for s in (1, 3):
            p2[s - 1].wait_recv()
            p3[s] = post(prec.at[band(s)], prec.at[band(s)], sibling)
        began[True, 1] = match_band(True, 1)
        began[True, 3] = match_band(True, 3)
        p3[1].wait_recv()
        began[False, 1] = match_band(False, 1)
        p2[1].wait_recv()
        p3[2] = post(prec.at[band(2)], prec.at[band(2)], sibling)
        p3[3].wait_recv()
        began[False, 3] = match_band(False, 3)
        until(NCH)
        began[True, 2] = match_band(True, 2)
        p3[2].wait_recv()
        began[False, 2] = match_band(False, 2)

        if CHAIN:
            for (mine_half, s), seen in began.items():
                if seen < NCH:
                    first = first_chunk(mine_half, s)

                    def late(j, _, first=first, seen=seen):
                        i = first + j

                        @pl.when(lax.rem(i + NZ * depth, NCH) >= seen)
                        def _():
                            match_one(i)

                        return 0

                    lax.fori_loop(0, 8, late, 0)
    else:
        load_bas.wait()
        load_hid.wait()
        until(NCH)

    if COL:
        prod = gm[...] * hm[...]
        pos = lax.broadcasted_iota(jnp.int32, (1, 128), 1)
        side = pos // 64
        p2nd = (pos // 16) % 4
        p1st = (pos // 4) % 4
        query = jnp.where(side == 0, p2nd * 2 + p1st // 2, p1st * 2 + p2nd // 2)
        sums = [jnp.sum(prod[s * SEQLEN:(s + 1) * SEQLEN], axis=0, keepdims=True) for s in (0, 1)]
        lane = lax.broadcasted_iota(jnp.int32, (8, 128), 1)
        line = lax.broadcasted_iota(jnp.int32, (8, 128), 0)
        tile = jnp.zeros((8, 128), f32)
        for s in (0, 1):
            for q in range(8):
                one = jnp.sum(jnp.where(query == q, sums[s], 0.0), axis=1, keepdims=True)
                tile = tile + jnp.where(jnp.logical_and(line == s, lane == q), one, 0.0)
        share[z] = tile / (SEQLEN * QLEN)
        zc = [remote(share.at[z], share.at[z], zs.at[s - 1], zr.at[s - 1], onz(s)) for s in range(1, LAYERS)]
        for copy in zc:
            copy.start()
        for copy in sent:
            copy.wait_send()
    if CHAIN:
        @pl.when(z > 0)
        def _():
            sends = pl.ds(0, NCH - NZ)
            remote(down.at[sends], rcv.at[sends], chain_s, chain_r.at[0], onz(LAYERS - 1)).wait_send()

        @pl.when(z < LAYERS - 1)
        def _():
            sends = pl.ds(0, NUP - NZ)
            remote(ups.at[sends], upr.at[sends], up_s, up_r.at[0], onz(1)).wait_send()

        @pl.when(z == LAYERS - 1)
        def _():
            remote(ups, upr, up_s, up_r.at[0], onz(1)).wait_send()

    if COL:
        for copy in zc:
            copy.wait_recv()
        total = share[0]
        for s in range(1, LAYERS):
            total = total + share[s]
        scores[...] = total[0:2, 0:8]
        for copy in zc:
            copy.wait_send()


def column(incoming, hidden, basis, eigvals, query_grads, query_hidden):
    hbm = pl.BlockSpec(memory_space=pltpu.HBM)
    vmem = pl.BlockSpec(memory_space=pltpu.VMEM)
    dma = pltpu.SemaphoreType.DMA
    section, scores = pl.pallas_call(
        kernel,
        out_shape=(
            pltpu.VMEM((1, 128, D), bf16),
            pltpu.VMEM((2, 8), f32),
        ),
        in_specs=[hbm, hbm, hbm, vmem, vmem, vmem],
        out_specs=(vmem, vmem),
        scratch_shapes=[
            pltpu.VMEM((128, D), bf16),
            pltpu.VMEM((NCH, 128, W), bf16),
            pltpu.VMEM((NCH, 128, W), bf16),
            pltpu.VMEM((NUP, 128, W), bf16),
            pltpu.VMEM((NUP, 128, W), bf16),
            pltpu.VMEM((128, F), bf16),
            pltpu.VMEM((D, 128), f32),
            pltpu.VMEM((16, D // 4), bf16),
            pltpu.VMEM((16, F // 4), bf16),
            pltpu.VMEM((64, D // 4), bf16),
            pltpu.VMEM((64, F // 4), bf16),
            pltpu.VMEM((128, D), bf16),
            pltpu.VMEM((128, F), bf16),
            pltpu.VMEM((4, 8, 128), f32),
            pltpu.VMEM((7, 8, 128), f32),
            pltpu.VMEM((4096, 128), bf16),
            pltpu.VMEM((4096, 128), bf16),
            pltpu.VMEM((4096, 128), f32),
            pltpu.VMEM((4096, 128), bf16),
            pltpu.VMEM((3, 1024, 128), bf16),
            pltpu.VMEM((1024, 128), bf16),
            pltpu.VMEM((3, 256, 128), bf16),
            pltpu.VMEM((D, 128), bf16),
            pltpu.VMEM((256, 256), bf16),
            pltpu.VMEM((128, 256), f32),
            pltpu.VMEM((128, 128), f32),
            pltpu.VMEM((128, 128), f32),
            pltpu.VMEM((LAYERS, 8, 128), f32),
            dma((3,)),
            dma,
            dma((NCH,)),
            dma,
            dma((NUP,)),
            dma((48,)),
            dma((48,)),
            dma((LAYERS - 1,)),
            dma((LAYERS - 1,)),
        ],
        compiler_params=pltpu.CompilerParams(
            collective_id=0, has_side_effects=True, vmem_limit_bytes=60 * 1024 * 1024
        ),
    )(incoming, hidden, basis, eigvals, query_grads, query_hidden)
    return section, scores


def solution(mesh):
    in_specs = (
        P("segment", "col", None),
        P("segment", "col", None),
        P("segment", None, "col"),
        P("segment", "col"),
        P("segment", "col", None),
        P("segment", "col", None),
    )
    out_specs = (P("segment", "col", None), P("col", None))
    return jax.shard_map(column, mesh=mesh, in_specs=in_specs, out_specs=out_specs, check_vma=False)
```

time: 113 us -> 79.6 us (0.70)
  the two profiles are of different devices: /device:TPU:40 before, /device:TPU:1 now
where the time goes in v2:
time: 79.6 us; the launch traced here: 79.5 us
  Pallas kernels  76.9 us (97%)
  local copies, waits for them, and re-layouts  1.88 us (2%)
    pallas_call x1, Pallas kernels, column(): pl.pallas_call(kernel, out_shape=(pltpu.VMEM((1, 128, D), bf16), pltpu.VM...  76.9 us
    unnamed x2, local copies, waits for them, and re-layouts  1.88 us

profile of v2, /device:TPU:1, one launch (start us, length us, event | category | flops | bytes accessed | tf_op | source)
XLA Modules:
  0.0 79.5 jit_solution(3459146567543881480)
XLA Ops:
  0.6 76.9 %shard_map.77 = (bf16[1,128,8192]{2,1,0:T(8,128)(2,1)S(1)}, f32[2,8]{1,0:T(2,128)S(1)}) custom-call(bf16[1,128,8192]{2,1,0:T(8,128)(2,1)} %inc.1, bf16[1,128,14336]{2,1,0:T(8,128)(2,1)} %hid.1, f32[1,8192,128]{2,1,0:T(8,128)} %bas.1, f32[1,128]{1,0:T(1,128)} %eig.1, bf16[1,4,8192]{2,1,0:T(4,128)(2,1)} %qg.1, bf16[1,4,14336]{2,1,0:T(4,128)(2,1)} %qh.1), custom_call_target="tpu_custom_call" | custom-call | tf_op jit(solution)/shard_map/pallas_call | solution.py:507
  77.6 1.3 %copy.10 = bf16[1,128,8192]{2,1,0:T(8,128)(2,1)} copy(bf16[1,128,8192]{2,1,0:T(8,128)(2,1)S(1)} %get-tuple-element.2) | data formatting | bytes 4194304
  78.9 0.6 copy.11

commit v3 on v2

--- a/solution.py
+++ b/solution.py
@@ -15,10 +15,14 @@
 LAYERS = 8
 W = 128
 NCH = D // W
-NZ = 6
+NZ = 8
 NUP = NZ * (LAYERS - 1)
-T_G1, T_H1, T_G2, T_G3, T_H2, T_R1, T_R2, T_P1, T_P2 = 6, 9, 15, 20, 32, 42, 47, 53, 61
-PER_P = 4
+T_G1, T_H1, T_H2S, T_G2, T_G3, T_H2, T_H3 = 8, 10, 15, 22, 24, 35, 37
+T_R1 = (38, 42)
+T_R2 = (43, 47)
+T_P1 = (48, 52)
+T_P2 = (56, 60)
+PER_P = 8
 CHAIN = True
 COL = True
 
@@ -140,7 +144,7 @@
         def _():
             out[0, :, lanes(i)] = down[i]
 
-        @pl.when(jnp.logical_and(partial, t // NZ >= 4))
+        @pl.when(jnp.logical_and(partial, t // NZ >= LAYERS // 2))
         def _():
             out[0, :, lanes(i)] = add(down[i], upr[i - (NCH - NUP)])
 
@@ -264,10 +268,10 @@
             copy.wait_recv()
         ebs[2] = ebs[1] + ebr[3] + ebr[4] + ebr[5]
         e3 = post(ebs.at[2], ebr.at[6], sibling)
+        until(T_H2S)
+        h2, h3 = gather2(qhv)
         until(T_G2)
-        h2, h3 = gather2(qhv)
-        for s, t in zip((1, 3, 2), (T_G2, T_G2 + 1, T_G2 + 2)):
-            until(t)
+        for s in (1, 3, 2):
             g2[s - 1].wait_recv()
             g3.append(post(qgv.at[rows16(s)], qgv.at[rows16(s)], sibling))
         until(T_G3)
@@ -301,153 +305,164 @@
             both = jnp.dot(jnp.concatenate([hi, lo], axis=1), wmat[...], preferred_element_type=f32)
             return both[:, :128] + both[:, 128:]
 
-        pair = []
-        for b in (1, 3, 2, 0):
-            block = lax.rem(a2 + b, 4)
-
-            def give(j, block=block):
-                for k in range(2):
-                    row = block * 1024 + (2 * j + k) * KB
-                    part_out[pl.ds(pl.multiple_of(row, KB), KB)] = expand((1 - c) * 4096 + row).astype(bf16)
-
-            slots(1, give)
-            at = pl.ds(pl.multiple_of(block * 1024, 1024), 1024)
-            pair.append(post(part_out.at[at], part_in.at[at], sibling))
-
-        r1 = []
-        for arrival, s in zip(pair, (1, 3, 2, 0)):
-            block = lax.rem(a1 + s, 4)
-
-            def keep(j, block=block):
-                for k in range(2):
-                    row = block * 1024 + (2 * j + k) * KB
-                    mine[pl.ds(pl.multiple_of(row, KB), KB)] = expand(c * 4096 + row)
-
-            slots(1, keep)
-            arrival.wait_recv()
-            at = pl.ds(pl.multiple_of(block * 1024, 1024), 1024)
-            total = mine[at] + part_in[at].astype(f32)
-            if s:
-                r1s[at] = total.astype(bf16)
-                r1.append(post(r1s.at[at], r1r.at[s - 1], on1(s)))
-            else:
-                mine[at] = total
+        def block_rows(block, half):
+            return pl.ds(pl.multiple_of(block * 1024 + half * KB, KB), KB)
+
+        pair = {}
+        for half in (0, 1):
+            slots(1)
+            for s in (1, 3, 2, 0):
+                block = lax.rem(a2 + s, 4)
+                at = block_rows(block, half)
+                part_out[at] = expand((1 - c) * 4096 + block * 1024 + half * KB).astype(bf16)
+                pair[half, s] = post(part_out.at[at], part_in.at[at], sibling)
+
+        r1 = {}
+        for half in (0, 1):
+            slots(1)
+            for s in (1, 3, 2, 0):
+                block = lax.rem(a1 + s, 4)
+                at = block_rows(block, half)
+                own_part = expand(c * 4096 + block * 1024 + half * KB)
+                pair[half, s].wait_recv()
+                total = own_part + part_in[at].astype(f32)
+                if s:
+                    r1s[at] = total.astype(bf16)
+                    r1[half, s] = post(r1s.at[at], r1r.at[s - 1, pl.ds(half * KB, KB)], on1(s))
+                else:
+                    mine[pl.ds(half * KB, KB)] = total
+
+        def match_hidden(j):
+            for k in range(4):
+                at = pl.ds(pl.multiple_of((4 * j + k) * 512, 512), 512)
+                hm[...] += lax.dot_general(
+                    hidv[:, at], qhv[:, at], (((1,), (1,)), ((), ())), preferred_element_type=f32
+                )
+
+        r2, p1, p2, p3 = {}, {}, {}, {}
+
+        def sum_first(half):
+            for s in (1, 2, 3):
+                r1[half, s].wait_recv()
+            for s in (1, 3, 2, 0):
+                at = pl.ds(pl.multiple_of(half * KB + lax.rem(a2 + s, 4) * 128, 128), 128)
+                total = mine[at] + r1r[0, at].astype(f32) + r1r[1, at].astype(f32) + r1r[2, at].astype(f32)
+                if s:
+                    r2s[at] = total.astype(bf16)
+                    r2[half, s] = post(r2s.at[at], r2r.at[s - 1, pl.ds(half * 128, 128)], on2(s))
+                else:
+                    mine[at] = total
+
+        def sum_second(half):
+            for s in (1, 2, 3):
+                r2[half, s].wait_recv()
+            at = pl.ds(pl.multiple_of(half * KB + a2 * 128, 128), 128)
+            got = pl.ds(half * 128, 128)
+            total = mine[at] + r2r[0, got].astype(f32) + r2r[1, got].astype(f32) + r2r[2, got].astype(f32)
+            rows = pl.ds(pl.multiple_of(c * 4096 + a1 * 1024 + half * KB + a2 * 128, 128), 128)
+            prec[rows] = total.astype(bf16)
+            for s in (1, 3, 2):
+                p1[half, s] = post(prec.at[rows], prec.at[rows], on2(s))
+
+        def band(s, half):
+            return pl.ds(pl.multiple_of(c * 4096 + lax.rem(a1 + 4 - s, 4) * 1024 + half * KB, KB), KB)
+
+        def gather_first(half):
+            for s in (1, 2, 3):
+                p1[half, s].wait_recv()
+            rows = band(0, half)
+            for s in (1, 3, 2):
+                p2[half, s] = post(prec.at[rows], prec.at[rows], on1(s))
+            p3[half, 0] = post(prec.at[rows], prec.at[rows], sibling)
+
+        def gather_second(half):
+            for s in (1, 3, 2):
+                rows = band(s, half)
+                p2[half, s].wait_recv()
+                p3[half, s] = post(prec.at[rows], prec.at[rows], sibling)
 
         until(T_H2)
         for s in (1, 3, 2):
             h2[s - 1].wait_recv()
             h3.append(post(qhv.at[rows16(s)], qhv.at[rows16(s)], sibling))
-            slots(1)
+        until(T_R1[0])
+        sum_first(0)
         load_hid.wait()
         for copy in h3:
             copy.wait_recv()
         hm[...] = jnp.zeros_like(hm)
-
-        def match_hidden(j):
-            for half in range(4):
-                at = pl.ds(pl.multiple_of((4 * j + half) * 512, 512), 512)
-                hm[...] += lax.dot_general(
-                    hidv[:, at], qhv[:, at], (((1,), (1,)), ((), ())), preferred_element_type=f32
-                )
-
-        slots(F // 2048, match_hidden)
-
-        until(T_R1)
-        for copy in r1:
-            copy.wait_recv()
-        r2 = []
-        for s in (1, 3, 2, 0):
-            sub = lax.rem(a2 + s, 4)
-            at = pl.ds(pl.multiple_of(sub * 256, 256), 256)
-            row = pl.ds(pl.multiple_of(a1 * 1024 + sub * 256, 256), 256)
-            total = mine[row] + r1r[0, at].astype(f32) + r1r[1, at].astype(f32) + r1r[2, at].astype(f32)
-            if s:
-                r2s[at] = total.astype(bf16)
-                r2.append(post(r2s.at[at], r2r.at[s - 1], on2(s)))
+        slots(4, match_hidden)
+        until(T_R1[1])
+        sum_first(1)
+        until(T_R2[0])
+        sum_second(0)
+        slots(3, lambda j: match_hidden(j + 4))
+        until(T_R2[1])
+        sum_second(1)
+        until(T_P1[0])
+        gather_first(0)
+        until(T_P1[1])
+        gather_first(1)
+
+        gm[...] = jnp.zeros_like(gm)
+        GROUP = KB // W
+
+        def match_group(first):
+            features = pl.ds(pl.multiple_of(first * W, KB), KB)
+            gm[...] += jnp.dot(out[0, :, features], prec[features], preferred_element_type=f32)
+
+        def first_chunk(own_side, s, half):
+            side, at = (c, a1) if own_side else (1 - c, a2)
+            return side * (NCH // 2) + lax.rem(at + 4 - s, 4) * 8 + half * GROUP
+
+        def done_at(first):
+            t = lax.rem(first + NZ * depth, NCH)
+            other = NZ * (LAYERS - 1 - t // NZ) + lax.rem(t, NZ)
+            return jnp.where(t < NZ * depth, jnp.maximum(t, other), t) + GROUP - 1
+
+        cutoff = T_P2[0]
+
+        def early(own_side, half):
+            def one(j):
+                first = first_chunk(own_side, j, half)
+
+                @pl.when(done_at(first) < cutoff)
+                def _():
+                    match_group(first)
+
+            if CHAIN and now[0] < NCH:
+                slots(4, one)
             else:
-                mine[row] = total
-        until(T_R2)
-        for copy in r2:
-            copy.wait_recv()
-        row = pl.ds(pl.multiple_of(a1 * 1024 + a2 * 256, 256), 256)
-        total = mine[row] + r2r[0].astype(f32) + r2r[1].astype(f32) + r2r[2].astype(f32)
-        own_rows = pl.ds(pl.multiple_of(c * 4096 + a1 * 1024 + a2 * 256, 256), 256)
-        prec[own_rows] = total.astype(bf16)
-        p1 = [post(prec.at[own_rows], prec.at[own_rows], on2(s)) for s in (1, 2, 3)]
-        until(T_P1)
-        for copy in p1:
-            copy.wait_recv()
-
-        def band(s):
-            return pl.ds(pl.multiple_of(c * 4096 + lax.rem(a1 + 4 - s, 4) * 1024, 1024), 1024)
-
-        p2 = [post(prec.at[band(0)], prec.at[band(0)], on1(s)) for s in (1, 2, 3)]
-        p3 = {0: post(prec.at[band(0)], prec.at[band(0)], sibling)}
-
-        gm[...] = jnp.zeros_like(gm)
-
-        def match_one(i):
-            gm[...] += jnp.dot(
-                out[0, :, lanes(i)], prec[pl.ds(pl.multiple_of(i * W, W), W)], preferred_element_type=f32
-            )
-
-        def first_chunk(mine_half, s):
-            side, at = (c, a1) if mine_half else (1 - c, a2)
-            return side * (NCH // 2) + lax.rem(at + 4 - s, 4) * 8
-
-        def match_band(mine_half, s, wait=0):
-            first = first_chunk(mine_half, s)
-            seen = now[0]
-
-            def pair_of(j):
-                for k in (0, 1):
-                    i = first + 2 * j + k
-                    if seen >= NCH or not CHAIN:
-                        match_one(i)
-                    else:
-                        @pl.when(lax.rem(i + NZ * depth, NCH) < seen)
-                        def _(i=i):
-                            match_one(i)
-
-            slots(4, pair_of)
-            return seen
-
-        began = {}
-        began[True, 0] = match_band(True, 0)
-        p3[0].wait_recv()
-        began[False, 0] = match_band(False, 0)
-        until(T_P2)
-        for s in (1, 3):
-            p2[s - 1].wait_recv()
-            p3[s] = post(prec.at[band(s)], prec.at[band(s)], sibling)
-        began[True, 1] = match_band(True, 1)
-        began[True, 3] = match_band(True, 3)
-        p3[1].wait_recv()
-        began[False, 1] = match_band(False, 1)
-        p2[1].wait_recv()
-        p3[2] = post(prec.at[band(2)], prec.at[band(2)], sibling)
-        p3[3].wait_recv()
-        began[False, 3] = match_band(False, 3)
+                for j in range(4):
+                    match_group(first_chunk(own_side, j, half))
+
+        until(T_P2[0])
+        late = []
+        for half in (0, 1):
+            until(T_P2[half])
+            gather_second(half)
+            if half == 1:
+                until(NCH)
+            if now[0] < NCH and CHAIN:
+                late.append((True, half))
+            early(True, half)
+            for s in range(4):
+                p3[half, s].wait_recv()
+            if now[0] < NCH and CHAIN:
+                late.append((False, half))
+            early(False, half)
         until(NCH)
-        began[True, 2] = match_band(True, 2)
-        p3[2].wait_recv()
-        began[False, 2] = match_band(False, 2)
-
-        if CHAIN:
-            for (mine_half, s), seen in began.items():
-                if seen < NCH:
-                    first = first_chunk(mine_half, s)
-
-                    def late(j, _, first=first, seen=seen):
-                        i = first + j
-
-                        @pl.when(lax.rem(i + NZ * depth, NCH) >= seen)
-                        def _():
-                            match_one(i)
-
-                        return 0
-
-                    lax.fori_loop(0, 8, late, 0)
+        for own_side, half in late:
+            def finish(j, _, own_side=own_side, half=half):
+                first = first_chunk(own_side, j, half)
+
+                @pl.when(done_at(first) >= cutoff)
+                def _():
+                    match_group(first)
+
+                return 0
+
+            lax.fori_loop(0, 4, finish, 0)
     else:
         load_bas.wait()
         load_hid.wait()
@@ -530,7 +545,7 @@
             pltpu.VMEM((7, 8, 128), f32),
             pltpu.VMEM((4096, 128), bf16),
             pltpu.VMEM((4096, 128), bf16),
-            pltpu.VMEM((4096, 128), f32),
+            pltpu.VMEM((1024, 128), f32),
             pltpu.VMEM((4096, 128), bf16),
             pltpu.VMEM((3, 1024, 128), bf16),
             pltpu.VMEM((1024, 128), bf16),
@@ -546,8 +561,8 @@
             dma((NCH,)),
             dma,
             dma((NUP,)),
-            dma((48,)),
-            dma((48,)),
+            dma((72,)),
+            dma((72,)),
             dma((LAYERS - 1,)),
             dma((LAYERS - 1,)),
         ],

time: 79.6 us -> 74.8 us (0.940)
  Pallas kernels: 76.9 us -> 72.2 us
    pallas_call x1, Pallas kernels: 76.9 us -> 72.2 us  [column(): pl.pallas_call(kernel, out_shape=(pltpu.VMEM((1, 128, D), bf16), pltpu.VM...]
where the time goes in v3:
time: 74.8 us; the launch traced here: 74.7 us
  Pallas kernels  72.2 us (97%)
  local copies, waits for them, and re-layouts  1.88 us (3%)
    pallas_call x1, Pallas kernels, column(): pl.pallas_call(kernel, out_shape=(pltpu.VMEM((1, 128, D), bf16), pltpu.VM...  72.2 us
    unnamed x2, local copies, waits for them, and re-layouts  1.88 us

profile of v3, /device:TPU:1, one launch (start us, length us, event | category | flops | bytes accessed | tf_op | source)
XLA Modules:
  0.0 74.7 jit_solution(16393874231205907406)
XLA Ops:
  0.6 72.2 %shard_map.77 = (bf16[1,128,8192]{2,1,0:T(8,128)(2,1)S(1)}, f32[2,8]{1,0:T(2,128)S(1)}) custom-call(bf16[1,128,8192]{2,1,0:T(8,128)(2,1)} %inc.1, bf16[1,128,14336]{2,1,0:T(8,128)(2,1)} %hid.1, f32[1,8192,128]{2,1,0:T(8,128)} %bas.1, f32[1,128]{1,0:T(1,128)} %eig.1, bf16[1,4,8192]{2,1,0:T(4,128)(2,1)} %qg.1, bf16[1,4,14336]{2,1,0:T(4,128)(2,1)} %qh.1), custom_call_target="tpu_custom_call" | custom-call | tf_op jit(solution)/shard_map/pallas_call | solution.py:522
  72.8 1.3 %copy.10 = bf16[1,128,8192]{2,1,0:T(8,128)(2,1)} copy(bf16[1,128,8192]{2,1,0:T(8,128)(2,1)S(1)} %get-tuple-element.2) | data formatting | bytes 4194304
  74.2 0.6 copy.11

commit v4 on v3

v4 whole, which is shorter than its diff:
```python
import jax
import jax.numpy as jnp
from jax import lax
from jax.experimental import pallas as pl
from jax.experimental.pallas import tpu as pltpu
from jax.sharding import PartitionSpec as P

D = 8192
F = 14336
K = 4096
SEQLEN = 64
QLEN = 16
DAMP = 0.1

LAYERS = 8
W = 128
NCH = D // W
NZ = 8
NUP = NZ * (LAYERS - 1)
S_E, S_G1, S_H1, S_G2, S_H2, S_BIG, S_SMALL, N_S = range(8)
R_E1, R_E2, R_E3, R_G1, R_H1, R_G2, R_G3, R_H2, R_H3 = range(9)
R_PAIR, R_R1, R_R2, R_P1, R_P2, R_P3, N_R = range(9, 23, 2)
T_H1S, T_G1, T_H1, T_G2, T_G3, T_H2, T_H3 = 8, 10, 18, 22, 23, 40, 43
T_R1 = (39, 43)
T_R2 = (45, 48)
T_P1 = (50, 54)
T_P2 = (59, 62)
PER_P = 8
STORES = 4
CHAIN = True
COL = True

f32 = jnp.float32
bf16 = jnp.bfloat16
MESH = pl.DeviceIdType.MESH


def remote(src, dst, ssem, rsem, dev):
    return pltpu.make_async_remote_copy(
        src_ref=src, dst_ref=dst, send_sem=ssem, recv_sem=rsem, device_id=dev, device_id_type=MESH
    )


def split(v):
    hi = v.astype(bf16)
    return hi, (v - hi.astype(f32)).astype(bf16)


def kernel(
    inc, hid, bas, eig, qg, qh,
    out, scores,
    own, down, rcv, ups, upr, fin, hidv, basv, bhl, eigv, qgr, qhr,
    g16, h16, a1g, a1h, qgv, qhv, ebs, ebr,
    part_out, part_in, kept, mine, r1s, r1r, r2s, r2r, prec,
    wmat, accp, gm, hm, share,
    ld_sem, out_sem, chain_s, chain_r, up_s, up_r, cs, cr, zs, zr,
):
    z = lax.axis_index("segment")
    col = lax.axis_index("col")
    c = lax.rem(col, 2)
    x = lax.rem(col // 2, 4)
    y = col // 8
    a1 = x + c * (y - x)
    a2 = y + c * (x - y)
    step1 = 2 + 6 * c
    step2 = 8 - 6 * c
    depth = LAYERS - 1 - z

    def on1(s):
        return (z, col + (lax.rem(a1 + s, 4) - a1) * step1)

    def on2(s):
        return (z, col + (lax.rem(a2 + s, 4) - a2) * step2)

    def onz(s):
        return (lax.rem(z + s, LAYERS), col)

    sibling = (z, col + 1 - 2 * c)

    barrier = pltpu.get_barrier_semaphore()
    greeted = [sibling] + [on1(s) for s in (1, 2, 3)] + [on2(s) for s in (1, 2, 3)]
    greeted += [onz(s) for s in range(1, LAYERS)]
    for dev in greeted:
        pl.semaphore_signal(barrier, inc=1, device_id=dev, device_id_type=MESH)

    load_own = pltpu.make_async_copy(inc.at[0], own, ld_sem.at[0])
    load_bas = pltpu.make_async_copy(bas.at[0], basv, ld_sem.at[1])
    load_hid = pltpu.make_async_copy(hid.at[0], hidv, ld_sem.at[2])
    small = [
        pltpu.make_async_copy(eig, eigv, ld_sem.at[3]),
        pltpu.make_async_copy(qg, qgr, ld_sem.at[4]),
        pltpu.make_async_copy(qh, qhr, ld_sem.at[5]),
    ]
    for copy in small + [load_own, load_bas, load_hid]:
        copy.start()
    for copy in small:
        copy.wait()

    def fold(q, wide):
        rows = q[0].astype(f32)
        return jnp.concatenate([rows[:, s * wide:(s + 1) * wide] for s in range(4)], axis=0).astype(bf16)

    g16[...] = fold(qgr, D // 4)
    h16[...] = fold(qhr, F // 4)
    ebs[0] = jnp.broadcast_to(eigv[...], (8, 128))
    pl.semaphore_wait(barrier, len(greeted))

    def post(src, dst, dev, send, recv):
        copy = remote(src, dst, cs.at[send], cr.at[recv], dev)
        copy.start()

    def arrived(like, recv):
        remote(like, like, cs.at[0], cr.at[recv], sibling).wait_recv()

    def link(i, t):
        return remote(down.at[i], rcv.at[i], chain_s, chain_r.at[t], onz(LAYERS - 1))

    def uplink(n):
        return remote(ups.at[pl.ds(n, 2)], upr.at[pl.ds(n, 2)], up_s, up_r.at[n // 2], onz(1))

    def lanes(i):
        return pl.ds(pl.multiple_of(i * W, W), W)

    def add(p, q):
        return (p.astype(f32) + q.astype(f32)).astype(bf16)

    def finish_chunk(i, value):
        fin[:, lanes(i)] = value
        pltpu.make_async_copy(fin.at[:, lanes(i)], out.at[0, :, lanes(i)], out_sem).start()

    def chunk_at(t):
        return lax.rem(t + NCH - NZ * depth, NCH)

    def chain_step(t):
        i = chunk_at(t)
        fed = jnp.logical_and(z < LAYERS - 1, t >= NZ)

        @pl.when(fed)
        def _():
            link(i, t - NZ).wait_recv()
            down[i] = add(own[:, lanes(i)], rcv[i])

        @pl.when(jnp.logical_not(fed))
        def _():
            down[i] = own[:, lanes(i)]

        @pl.when(jnp.logical_and(z > 0, t < NCH - NZ))
        def _():
            link(i, t).start()

        partial = t < NZ * depth

        @pl.when(jnp.logical_not(partial))
        def _():
            finish_chunk(i, down[i])

        @pl.when(jnp.logical_and(partial, t // NZ >= LAYERS // 2))
        def _():
            finish_chunk(i, add(down[i], upr[i - (NCH - NUP)]))

    def up_step(t):
        hop = t // NZ
        cut = lax.rem(z - hop + LAYERS, LAYERS)

        @pl.when(jnp.logical_and(cut > 0, lax.rem(t, 2) == 0))
        def _():
            n = (cut - 1) * NZ + t - hop * NZ
            i = NCH - NUP + n
            last = hop == LAYERS - 1
            two = pl.ds(n, 2)

            @pl.when(hop > 0)
            def _():
                uplink(n).wait_recv()

            @pl.when(jnp.logical_and(z >= cut, hop > 0))
            def _():
                for k in (0, 1):
                    ups[n + k] = add(own[:, lanes(i + k)], upr[n + k])

            @pl.when(jnp.logical_and(z >= cut, hop == 0))
            def _():
                for k in (0, 1):
                    ups[n + k] = own[:, lanes(i + k)]

            @pl.when(jnp.logical_and(z < cut, jnp.logical_not(last)))
            def _():
                ups[two] = upr[two]

            @pl.when(jnp.logical_not(last))
            def _():
                uplink(n).start()

            @pl.when(jnp.logical_and(z < cut, cut - z <= LAYERS // 2))
            def _():
                for k in (0, 1):
                    finish_chunk(i + k, add(down[i + k], upr[n + k]))

    now = [0]

    def slots(n, fn=None):
        if not CHAIN:
            now[0] = max(now[0], min(now[0] + n, NCH))
            if fn is not None:
                def plain(j, _):
                    fn(j)
                    return 0

                lax.fori_loop(0, n, plain, 0)
            return
        done = 0
        while done < n:
            base = now[0]
            stop = n - done
            if base < NZ * LAYERS:
                stop = min(stop, NZ * LAYERS - base)
            elif base < NCH:
                stop = min(stop, NCH - base)
            elif fn is None:
                return

            def step(j, _, base=base, done=done):
                if base < NCH:
                    chain_step(base + j)
                if base < NZ * LAYERS:
                    up_step(base + j)
                if fn is not None:
                    fn(done + j)
                return 0

            lax.fori_loop(0, stop, step, 0)
            now[0] += stop
            done += stop

    def until(t):
        if now[0] < t:
            slots(t - now[0])

    if COL:
        for s in (1, 2, 3):
            post(ebs.at[0], ebr.at[s - 1], on1(s), S_E, R_E1)
        for s in (2, 1, 3):
            post(g16, a1g.at[pl.ds(a1 * 16, 16)], on1(s), S_G1, R_G1)

    load_own.wait()

    def order16():
        r = lax.broadcasted_iota(jnp.int32, (64, 64), 0)
        k = lax.broadcasted_iota(jnp.int32, (64, 64), 1)
        src = ((r % 16) // 4) * 16 + (r // 16) * 4 + r % 4
        return (k == src).astype(f32).astype(bf16)

    def rows16(s):
        return pl.ds(pl.multiple_of(c * 64 + lax.rem(a2 + 4 - s, 4) * 16, 16), 16)

    def assemble(a, q, wide):
        part = jnp.dot(order16(), a[...], preferred_element_type=f32).astype(bf16)
        for s in range(4):
            q[rows16(0), s * wide:(s + 1) * wide] = part[s * 16:(s + 1) * 16]

    def share_rows(q, s, dev, send, recv):
        post(q.at[rows16(s)], q.at[rows16(s)], dev, send, recv)

    if COL:
        a1g[pl.ds(pl.multiple_of(a1 * 16, 16), 16)] = g16[...]
        a1h[pl.ds(pl.multiple_of(a1 * 16, 16), 16)] = h16[...]
        until(T_H1S)
        for s in (2, 1, 3):
            post(h16, a1h.at[pl.ds(a1 * 16, 16)], on1(s), S_H1, R_H1)
        until(T_G1)
        arrived(ebr.at[0:3], R_E1)
        ebs[1] = ebs[0] + ebr[0] + ebr[1] + ebr[2]
        for s in (1, 2, 3):
            post(ebs.at[1], ebr.at[2 + s], on2(s), S_E, R_E2)
        arrived(a1g.at[0:48], R_G1)
        assemble(a1g, qgv, D // 4)
        for s in (2, 1, 3):
            share_rows(qgv, 0, on2(s), S_G2, R_G2)
        share_rows(qgv, 0, sibling, S_G2, R_G3)

        KB = 512
        load_bas.wait()

        def split_basis(j):
            for k in (0, 1):
                at = pl.ds(pl.multiple_of((2 * j + k) * KB, KB), KB)
                hi, lo = split(basv[at])
                bhl[at, 0:128] = hi
                bhl[at, 128:256] = lo

        slots(8, split_basis)
        until(T_H1)
        arrived(a1h.at[0:48], R_H1)
        assemble(a1h, qhv, F // 4)
        for s in (2, 1, 3):
            share_rows(qhv, 0, on2(s), S_H2, R_H2)
        share_rows(qhv, 0, sibling, S_H2, R_H3)
        arrived(ebr.at[3:6], R_E2)
        ebs[2] = ebs[1] + ebr[3] + ebr[4] + ebr[5]
        post(ebs.at[2], ebr.at[6], sibling, S_E, R_E3)
        until(T_G2)
        arrived(qgv.at[0:48], R_G2)
        for s in (1, 2, 3):
            share_rows(qgv, s, sibling, S_G2, R_G3)
        until(T_G3)
        arrived(qgv.at[0:64], R_G3)
        arrived(ebr.at[6:7], R_E3)
        ebs[3] = ebs[2] + ebr[6]

        accp[...] = jnp.zeros_like(accp)

        def project(j):
            for k in range(PER_P):
                at = pl.ds(pl.multiple_of((PER_P * j + k) * KB, KB), KB)
                accp[...] += jnp.dot(qgv[:, at], bhl[at], preferred_element_type=f32)

        slots(D // KB // PER_P, project)
        damping = DAMP * jnp.sum(ebs[3][0:1], axis=1, keepdims=True) / K
        weighted = (accp[:, :128] + accp[:, 128:]) / (eigv[...] + damping)
        hi, lo = split(weighted.T)
        wmat[0:128, 0:128] = hi
        wmat[128:256, 0:128] = hi
        wmat[0:128, 128:256] = lo
        wmat[128:256, 128:256] = jnp.zeros_like(lo)

        def expand(side, half):
            at = pl.ds(pl.multiple_of(side * 4096 + half * 2048, 2048), 2048)
            both = jnp.dot(bhl[at], wmat[...], preferred_element_type=f32)
            return both[:, :128] + both[:, 128:]

        def block_rows(block, half):
            return pl.ds(pl.multiple_of(half * 2048 + block * KB, KB), KB)

        def give(half):
            at = pl.ds(half * 2048, 2048)
            part_out[at] = expand(1 - c, half).astype(bf16)
            post(part_out.at[at], part_in.at[at], sibling, S_BIG, R_PAIR + half)

        def keep(half):
            kept[...] = expand(c, half)
            arrived(part_in.at[0:2048], R_PAIR + half)
            for s in (2, 1, 3, 0):
                block = lax.rem(a1 + s, 4)
                at = block_rows(block, half)
                total = kept[pl.ds(pl.multiple_of(block * KB, KB), KB)] + part_in[at].astype(f32)
                if s:
                    r1s[at] = total.astype(bf16)
                    post(r1s.at[at], r1r.at[s - 1, pl.ds(half * KB, KB)], on1(s), S_BIG, R_R1 + half)
                else:
                    mine[pl.ds(half * KB, KB)] = total

        give(0)
        slots(1)
        give(1)
        keep(0)
        slots(1)
        keep(1)

        def match_hidden(j):
            for k in range(4):
                at = pl.ds(pl.multiple_of((4 * j + k) * 512, 512), 512)
                hm[...] += lax.dot_general(
                    hidv[:, at], qhv[:, at], (((1,), (1,)), ((), ())), preferred_element_type=f32
                )

        def sum_first(half):
            arrived(prec.at[0:3 * KB], R_R1 + half)
            for s in (2, 1, 3, 0):
                at = pl.ds(pl.multiple_of(half * KB + lax.rem(a2 + s, 4) * 128, 128), 128)
                total = mine[at] + r1r[0, at].astype(f32) + r1r[1, at].astype(f32) + r1r[2, at].astype(f32)
                if s:
                    r2s[at] = total.astype(bf16)
                    post(r2s.at[at], r2r.at[s - 1, pl.ds(half * 128, 128)], on2(s), S_SMALL, R_R2 + half)
                else:
                    mine[at] = total

        def sum_second(half):
            arrived(prec.at[0:384], R_R2 + half)
            at = pl.ds(pl.multiple_of(half * KB + a2 * 128, 128), 128)
            got = pl.ds(half * 128, 128)
            total = mine[at] + r2r[0, got].astype(f32) + r2r[1, got].astype(f32) + r2r[2, got].astype(f32)
            rows = pl.ds(pl.multiple_of(c * 4096 + half * 2048 + a1 * KB + a2 * 128, 128), 128)
            prec[rows] = total.astype(bf16)
            for s in (2, 1, 3):
                post(prec.at[rows], prec.at[rows], on2(s), S_SMALL, R_P1 + half)

        def band(s, half):
            return pl.ds(pl.multiple_of(c * 4096 + half * 2048 + lax.rem(a1 + 4 - s, 4) * KB, KB), KB)

        def gather_first(half):
            arrived(prec.at[0:384], R_P1 + half)
            rows = band(0, half)
            for s in (2, 1, 3):
                post(prec.at[rows], prec.at[rows], on1(s), S_BIG, R_P2 + half)
            post(prec.at[rows], prec.at[rows], sibling, S_BIG, R_P3 + half)

        def gather_second(half):
            arrived(prec.at[0:3 * KB], R_P2 + half)
            for s in (1, 2, 3):
                rows = band(s, half)
                post(prec.at[rows], prec.at[rows], sibling, S_BIG, R_P3 + half)

        until(T_R1[0])
        sum_first(0)
        until(T_H2)
        arrived(qhv.at[0:48], R_H2)
        for s in (1, 2, 3):
            share_rows(qhv, s, sibling, S_H2, R_H3)
        until(T_R1[1])
        sum_first(1)
        until(T_H3)
        load_hid.wait()
        arrived(qhv.at[0:64], R_H3)
        hm[...] = jnp.zeros_like(hm)
        slots(2, match_hidden)
        until(T_R2[0])
        sum_second(0)
        slots(2, lambda j: match_hidden(j + 2))
        until(T_R2[1])
        sum_second(1)
        slots(2, lambda j: match_hidden(j + 4))
        until(T_P1[0])
        gather_first(0)
        slots(1, lambda j: match_hidden(j + 6))
        until(T_P1[1])
        gather_first(1)

        gm[...] = jnp.zeros_like(gm)
        GROUP = KB // W

        def match_group(first):
            features = pl.ds(pl.multiple_of(first * W, KB), KB)
            gm[...] += jnp.dot(fin[:, features], prec[features], preferred_element_type=f32)

        def first_chunk(own_side, s, half):
            side, at = (c, a1) if own_side else (1 - c, a2)
            return side * (NCH // 2) + half * (NCH // 4) + lax.rem(at + 4 - s, 4) * GROUP

        def done_at(first):
            t = lax.rem(first + NZ * depth, NCH)
            other = NZ * (LAYERS - 1 - t // NZ) + lax.rem(t, NZ)
            return jnp.where(t < NZ * depth, jnp.maximum(t, other), t) + GROUP - 1

        cutoff = T_P2[0]

        def early(own_side, half):
            def one(j):
                first = first_chunk(own_side, j, half)

                @pl.when(done_at(first) < cutoff)
                def _():
                    match_group(first)

            if CHAIN and now[0] < NCH:
                slots(4, one)
            else:
                for j in range(4):
                    match_group(first_chunk(own_side, j, half))

        until(T_P2[0])
        late = []
        for half in (0, 1):
            until(T_P2[half])
            gather_second(half)
            if half == 1:
                until(NCH)
            if now[0] < NCH and CHAIN:
                late.append((True, half))
            early(True, half)
            arrived(prec.at[0:2048], R_P3 + half)
            if now[0] < NCH and CHAIN:
                late.append((False, half))
            early(False, half)
        until(NCH)
        for own_side, half in late:
            for j in range(4):
                first = first_chunk(own_side, j, half)

                @pl.when(done_at(first) >= cutoff)
                def _(first=first):
                    match_group(first)
    else:
        load_bas.wait()
        load_hid.wait()
        until(NCH)

    if COL:
        prod = gm[...] * hm[...]
        pos = lax.broadcasted_iota(jnp.int32, (128, 128), 0)
        side = pos // 64
        p2nd = (pos // 16) % 4
        p1st = (pos // 4) % 4
        query = jnp.where(side == 0, p2nd * 2 + p1st // 2, p1st * 2 + p2nd // 2)
        pick = (query == lax.broadcasted_iota(jnp.int32, (128, 128), 1)).astype(f32)
        sums = [jnp.sum(prod[s * SEQLEN:(s + 1) * SEQLEN], axis=0, keepdims=True) for s in (0, 1)]
        line = lax.broadcasted_iota(jnp.int32, (8, 128), 0)
        both = jnp.where(line == 0, sums[0], jnp.where(line == 1, sums[1], 0.0))
        tile = jnp.dot(both, pick, precision=lax.Precision.HIGHEST, preferred_element_type=f32)
        share[z] = tile / (SEQLEN * QLEN)
        for s in (4, 3, 5, 2, 6, 1, 7):
            remote(share.at[z], share.at[z], zs, zr, onz(s)).start()
        for like, kind in (
            (ebr, S_E),
            (a1g.at[0:48], S_G1),
            (a1h.at[0:48], S_H1),
            (qgv.at[0:112], S_G2),
            (qhv.at[0:112], S_H2),
            (bhl.at[0:7168], S_BIG),
            (prec.at[0:1536], S_SMALL),
        ):
            remote(like, like, cs.at[kind], cr.at[0], sibling).wait_send()
    if CHAIN:
        pltpu.make_async_copy(fin, out.at[0], out_sem).wait()

        @pl.when(z > 0)
        def _():
            sends = pl.ds(0, NCH - NZ)
            remote(down.at[sends], rcv.at[sends], chain_s, chain_r.at[0], onz(LAYERS - 1)).wait_send()

        @pl.when(z < LAYERS - 1)
        def _():
            sends = pl.ds(0, NUP - NZ)
            remote(ups.at[sends], upr.at[sends], up_s, up_r.at[0], onz(1)).wait_send()

        @pl.when(z == LAYERS - 1)
        def _():
            remote(ups, upr, up_s, up_r.at[0], onz(1)).wait_send()

    if COL:
        others = remote(share.at[0:LAYERS - 1], share.at[0:LAYERS - 1], zs, zr, sibling)
        others.wait_recv()
        total = share[0]
        for s in range(1, LAYERS):
            total = total + share[s]
        scores[...] = total[0:2, 0:8]
        others.wait_send()


def store(section, scores, section_out, scores_out, sem):
    rows = 128 // STORES
    copies = [
        pltpu.make_async_copy(section.at[0, pl.ds(k * rows, rows)], section_out.at[0, pl.ds(k * rows, rows)], sem.at[k])
        for k in range(STORES)
    ]
    copies.append(pltpu.make_async_copy(scores, scores_out, sem.at[STORES]))
    for copy in copies:
        copy.start()
    for copy in copies:
        copy.wait()


def column(incoming, hidden, basis, eigvals, query_grads, query_hidden):
    hbm = pl.BlockSpec(memory_space=pltpu.HBM)
    vmem = pl.BlockSpec(memory_space=pltpu.VMEM)
    dma = pltpu.SemaphoreType.DMA
    section, scores = pl.pallas_call(
        kernel,
        out_shape=(
            pltpu.VMEM((1, 128, D), bf16),
            pltpu.VMEM((2, 8), f32),
        ),
        in_specs=[hbm] * 6,
        out_specs=(pl.BlockSpec(memory_space=pl.ANY), vmem),
        scratch_shapes=[
            pltpu.VMEM((128, D), bf16),
            pltpu.VMEM((NCH, 128, W), bf16),
            pltpu.VMEM((NCH, 128, W), bf16),
            pltpu.VMEM((NUP, 128, W), bf16),
            pltpu.VMEM((NUP, 128, W), bf16),
            pltpu.VMEM((128, D), bf16),
            pltpu.VMEM((128, F), bf16),
            pltpu.VMEM((D, 128), f32),
            pltpu.VMEM((D, 256), bf16),
            pltpu.VMEM((1, 128), f32),
            pltpu.VMEM((1, 4, D), bf16),
            pltpu.VMEM((1, 4, F), bf16),
            pltpu.VMEM((16, D // 4), bf16),
            pltpu.VMEM((16, F // 4), bf16),
            pltpu.VMEM((64, D // 4), bf16),
            pltpu.VMEM((64, F // 4), bf16),
            pltpu.VMEM((128, D), bf16),
            pltpu.VMEM((128, F), bf16),
            pltpu.VMEM((4, 8, 128), f32),
            pltpu.VMEM((7, 8, 128), f32),
            pltpu.VMEM((4096, 128), bf16),
            pltpu.VMEM((4096, 128), bf16),
            pltpu.VMEM((2048, 128), f32),
            pltpu.VMEM((1024, 128), f32),
            pltpu.VMEM((4096, 128), bf16),
            pltpu.VMEM((3, 1024, 128), bf16),
            pltpu.VMEM((1024, 128), bf16),
            pltpu.VMEM((3, 256, 128), bf16),
            pltpu.VMEM((D, 128), bf16),
            pltpu.VMEM((256, 256), bf16),
            pltpu.VMEM((128, 256), f32),
            pltpu.VMEM((128, 128), f32),
            pltpu.VMEM((128, 128), f32),
            pltpu.VMEM((LAYERS, 8, 128), f32),
            dma((6,)),
            dma,
            dma,
            dma((NCH - NZ,)),
            dma,
            dma((NUP // 2,)),
            dma((N_S,)),
            dma((N_R,)),
            dma,
            dma,
        ],
        compiler_params=pltpu.CompilerParams(
            collective_id=0, has_side_effects=True, vmem_limit_bytes=60 * 1024 * 1024
        ),
    )(incoming, hidden, basis, eigvals, query_grads, query_hidden)
    anyspace = pl.BlockSpec(memory_space=pl.ANY)
    return pl.pallas_call(
        store,
        out_shape=(
            jax.ShapeDtypeStruct((1, 128, D), bf16),
            jax.ShapeDtypeStruct((2, 8), f32),
        ),
        in_specs=[anyspace, anyspace],
        out_specs=(hbm, hbm),
        scratch_shapes=[dma((STORES + 1,))],
        compiler_params=pltpu.CompilerParams(vmem_limit_bytes=1024 * 1024),
    )(section, scores)


def solution(mesh):
    in_specs = (
        P("segment", "col", None),
        P("segment", "col", None),
        P("segment", None, "col"),
        P("segment", "col"),
        P("segment", "col", None),
        P("segment", "col", None),
    )
    out_specs = (P("segment", "col", None), P("col", None))
    return jax.shard_map(column, mesh=mesh, in_specs=in_specs, out_specs=out_specs, check_vma=False)
```

time: 74.8 us -> 65.3 us (0.87)
  Pallas kernels: 72.2 us -> 64.6 us
  local copies, waits for them, and re-layouts: 1.88 us -> 0 us
    pallas_call x1, Pallas kernels: 72.2 us -> 63.2 us  [column(): pl.pallas_call(kernel, out_shape=(pltpu.VMEM((1, 128, D), bf16), pltpu.VM...]
    unnamed x2 -> x0, local copies, waits for them, and re-layouts: 1.88 us -> none
    pallas_call x0 -> x1, Pallas kernels: none -> 1.36 us  [column(): pl.pallas_call(store, out_shape=(jax.ShapeDtypeStruct((1, 128, D), bf16),...]
where the time goes in v4:
time: 65.3 us; the launch traced here: 65.2 us
  Pallas kernels  64.6 us (99%)
    pallas_call x1, Pallas kernels, column(): pl.pallas_call(kernel, out_shape=(pltpu.VMEM((1, 128, D), bf16), pltpu.VM...  63.2 us
    pallas_call x1, Pallas kernels, column(): pl.pallas_call(store, out_shape=(jax.ShapeDtypeStruct((1, 128, D), bf16),...  1.36 us

profile of v4, /device:TPU:1, one launch (start us, length us, event | category | flops | bytes accessed | tf_op | source)
XLA Modules:
  0.0 65.2 jit_solution(596169719055911416)
XLA Ops:
  0.6 63.2 %shard_map.77 = (bf16[1,128,8192]{2,1,0:T(8,128)(2,1)S(1)}, f32[2,8]{1,0:T(2,128)S(1)}) custom-call(bf16[1,128,8192]{2,1,0:T(8,128)(2,1)} %inc.1, bf16[1,128,14336]{2,1,0:T(8,128)(2,1)} %hid.1, f32[1,8192,128]{2,1,0:T(8,128)} %bas.1, f32[1,128]{1,0:T(1,128)} %eig.1, bf16[1,4,8192]{2,1,0:T(4,128)(2,1)} %qg.1, bf16[1,4,14336]{2,1,0:T(4,128)(2,1)} %qh.1), custom_call_target="tpu_custom_call" | custom-call | tf_op jit(solution)/shard_map/pallas_call | solution.py:556
  63.9 1.4 %shard_map.78 = (bf16[1,128,8192]{2,1,0:T(8,128)(2,1)}, f32[2,8]{1,0:T(2,128)}) custom-call(bf16[1,128,8192]{2,1,0:T(8,128)(2,1)S(1)} %get-tuple-element.4.section, f32[2,8]{1,0:T(2,128)S(1)} %get-tuple-element.5.scores), custom_call_target="tpu_custom_call" | custom-call | tf_op jit(solution)/shard_map/pallas_call | solution.py:615

commit v5 on v4

--- a/solution.py
+++ b/solution.py
@@ -13,19 +13,24 @@
 DAMP = 0.1
 
 LAYERS = 8
-W = 128
+W = 256
 NCH = D // W
-NZ = 8
+NZ = 4
 NUP = NZ * (LAYERS - 1)
 S_E, S_G1, S_H1, S_G2, S_H2, S_BIG, S_SMALL, N_S = range(8)
-R_E1, R_E2, R_E3, R_G1, R_H1, R_G2, R_G3, R_H2, R_H3 = range(9)
-R_PAIR, R_R1, R_R2, R_P1, R_P2, R_P3, N_R = range(9, 23, 2)
-T_H1S, T_G1, T_H1, T_G2, T_G3, T_H2, T_H3 = 8, 10, 18, 22, 23, 40, 43
-T_R1 = (39, 43)
+R_E1, R_E2, R_E3, R_G1, R_H1, R_H2, R_H3 = range(7)
+R_G2, R_G3, R_PAIR, R_R1, R_R2, R_P1, R_P2, R_P3, N_R = range(7, 25, 2)
+SLOTS = 2 * NCH
+T_H1S, T_G1, T_H1, T_H2, T_H3 = 8, 10, 18, 43, 51
+T_G2 = (17, 21)
+T_G3 = (19, 23)
+T_R1 = (38, 42)
 T_R2 = (45, 48)
-T_P1 = (50, 54)
-T_P2 = (59, 62)
+T_P1 = (49, 51)
+T_P2 = (57, 60)
 PER_P = 8
+KB = 512
+HALF = D // 2
 STORES = 4
 CHAIN = True
 COL = True
@@ -116,7 +121,7 @@
         return remote(down.at[i], rcv.at[i], chain_s, chain_r.at[t], onz(LAYERS - 1))
 
     def uplink(n):
-        return remote(ups.at[pl.ds(n, 2)], upr.at[pl.ds(n, 2)], up_s, up_r.at[n // 2], onz(1))
+        return remote(ups.at[n], upr.at[n], up_s, up_r.at[n], onz(1))
 
     def lanes(i):
         return pl.ds(pl.multiple_of(i * W, W), W)
@@ -162,12 +167,11 @@
         hop = t // NZ
         cut = lax.rem(z - hop + LAYERS, LAYERS)
 
-        @pl.when(jnp.logical_and(cut > 0, lax.rem(t, 2) == 0))
+        @pl.when(cut > 0)
         def _():
             n = (cut - 1) * NZ + t - hop * NZ
             i = NCH - NUP + n
             last = hop == LAYERS - 1
-            two = pl.ds(n, 2)
 
             @pl.when(hop > 0)
             def _():
@@ -175,17 +179,15 @@
 
             @pl.when(jnp.logical_and(z >= cut, hop > 0))
             def _():
-                for k in (0, 1):
-                    ups[n + k] = add(own[:, lanes(i + k)], upr[n + k])
+                ups[n] = add(own[:, lanes(i)], upr[n])
 
             @pl.when(jnp.logical_and(z >= cut, hop == 0))
             def _():
-                for k in (0, 1):
-                    ups[n + k] = own[:, lanes(i + k)]
+                ups[n] = own[:, lanes(i)]
 
             @pl.when(jnp.logical_and(z < cut, jnp.logical_not(last)))
             def _():
-                ups[two] = upr[two]
+                ups[n] = upr[n]
 
             @pl.when(jnp.logical_not(last))
             def _():
@@ -193,44 +195,37 @@
 
             @pl.when(jnp.logical_and(z < cut, cut - z <= LAYERS // 2))
             def _():
-                for k in (0, 1):
-                    finish_chunk(i + k, add(down[i + k], upr[n + k]))
+                finish_chunk(i, add(down[i], upr[n]))
 
     now = [0]
 
     def slots(n, fn=None):
-        if not CHAIN:
-            now[0] = max(now[0], min(now[0] + n, NCH))
+        if CHAIN:
+            ahead = min(n, SLOTS - now[0])
+        else:
+            ahead = 0
+        base = now[0]
+
+        def step(j, _):
+            t = base + j
+
+            @pl.when(lax.rem(t, 2) == 0)
+            def _():
+                chain_step(t // 2)
+
+            @pl.when(lax.rem(t, 2) == 1)
+            def _():
+                up_step(t // 2)
+
             if fn is not None:
-                def plain(j, _):
-                    fn(j)
-                    return 0
-
-                lax.fori_loop(0, n, plain, 0)
-            return
-        done = 0
-        while done < n:
-            base = now[0]
-            stop = n - done
-            if base < NZ * LAYERS:
-                stop = min(stop, NZ * LAYERS - base)
-            elif base < NCH:
-                stop = min(stop, NCH - base)
-            elif fn is None:
-                return
-
-            def step(j, _, base=base, done=done):
-                if base < NCH:
-                    chain_step(base + j)
-                if base < NZ * LAYERS:
-                    up_step(base + j)
-                if fn is not None:
-                    fn(done + j)
-                return 0
-
-            lax.fori_loop(0, stop, step, 0)
-            now[0] += stop
-            done += stop
+                fn(j)
+            return 0
+
+        if ahead:
+            lax.fori_loop(0, ahead, step, 0)
+        if fn is not None and n > ahead:
+            lax.fori_loop(ahead, n, lambda j, _: (fn(j), 0)[1], 0)
+        now[0] = min(base + n, SLOTS)
 
     def until(t):
         if now[0] < t:
@@ -260,6 +255,10 @@
 
     def share_rows(q, s, dev, send, recv):
         post(q.at[rows16(s)], q.at[rows16(s)], dev, send, recv)
+
+    def share_half(s, half, dev, recv):
+        part = qgv.at[rows16(s), half * HALF:(half + 1) * HALF]
+        post(part, part, dev, S_G2, recv + half)
 
     if COL:
         a1g[pl.ds(pl.multiple_of(a1 * 16, 16), 16)] = g16[...]
@@ -274,11 +273,12 @@
             post(ebs.at[1], ebr.at[2 + s], on2(s), S_E, R_E2)
         arrived(a1g.at[0:48], R_G1)
         assemble(a1g, qgv, D // 4)
-        for s in (2, 1, 3):
-            share_rows(qgv, 0, on2(s), S_G2, R_G2)
-        share_rows(qgv, 0, sibling, S_G2, R_G3)
-
-        KB = 512
+        for half in (0, 1):
+            for s in (2, 1, 3):
+                share_half(0, half, on2(s), R_G2)
+        for half in (0, 1):
+            share_half(0, half, sibling, R_G3)
+
         load_bas.wait()
 
         def split_basis(j):
@@ -288,33 +288,44 @@
                 bhl[at, 0:128] = hi
                 bhl[at, 128:256] = lo
 
-        slots(8, split_basis)
+        accp[...] = jnp.zeros_like(accp)
+
+        def project(half):
+            arrived(qgv.at[0:64, 0:HALF], R_G3 + half)
+
+            def blocks(j):
+                for k in range(PER_P):
+                    at = pl.ds(pl.multiple_of(half * HALF + (PER_P * j + k) * KB, KB), KB)
+                    accp[...] += jnp.dot(qgv[:, at], bhl[at], preferred_element_type=f32)
+
+            slots(HALF // KB // PER_P, blocks)
+
+        def swap_half(half):
+            arrived(qgv.at[0:48, 0:HALF], R_G2 + half)
+            for s in (1, 2, 3):
+                share_half(s, half, sibling, R_G3)
+
+        slots(7, split_basis)
+        until(T_G2[0])
+        swap_half(0)
         until(T_H1)
         arrived(a1h.at[0:48], R_H1)
         assemble(a1h, qhv, F // 4)
         for s in (2, 1, 3):
             share_rows(qhv, 0, on2(s), S_H2, R_H2)
         share_rows(qhv, 0, sibling, S_H2, R_H3)
+        split_basis(7)
         arrived(ebr.at[3:6], R_E2)
         ebs[2] = ebs[1] + ebr[3] + ebr[4] + ebr[5]
         post(ebs.at[2], ebr.at[6], sibling, S_E, R_E3)
-        until(T_G2)
-        arrived(qgv.at[0:48], R_G2)
-        for s in (1, 2, 3):
-            share_rows(qgv, s, sibling, S_G2, R_G3)
-        until(T_G3)
-        arrived(qgv.at[0:64], R_G3)
+        until(T_G3[0])
+        project(0)
+        until(T_G2[1])
+        swap_half(1)
+        until(T_G3[1])
         arrived(ebr.at[6:7], R_E3)
         ebs[3] = ebs[2] + ebr[6]
-
-        accp[...] = jnp.zeros_like(accp)
-
-        def project(j):
-            for k in range(PER_P):
-                at = pl.ds(pl.multiple_of((PER_P * j + k) * KB, KB), KB)
-                accp[...] += jnp.dot(qgv[:, at], bhl[at], preferred_element_type=f32)
-
-        slots(D // KB // PER_P, project)
+        project(1)
         damping = DAMP * jnp.sum(ebs[3][0:1], axis=1, keepdims=True) / K
         weighted = (accp[:, :128] + accp[:, 128:]) / (eigv[...] + damping)
         hi, lo = split(weighted.T)
@@ -337,12 +348,13 @@
             post(part_out.at[at], part_in.at[at], sibling, S_BIG, R_PAIR + half)
 
         def keep(half):
-            kept[...] = expand(c, half)
+            kept[pl.ds(half * 2048, 2048)] = expand(c, half)
+
+        def add_pair(half):
             arrived(part_in.at[0:2048], R_PAIR + half)
             for s in (2, 1, 3, 0):
-                block = lax.rem(a1 + s, 4)
-                at = block_rows(block, half)
-                total = kept[pl.ds(pl.multiple_of(block * KB, KB), KB)] + part_in[at].astype(f32)
+                at = block_rows(lax.rem(a1 + s, 4), half)
+                total = kept[at] + part_in[at].astype(f32)
                 if s:
                     r1s[at] = total.astype(bf16)
                     post(r1s.at[at], r1r.at[s - 1, pl.ds(half * KB, KB)], on1(s), S_BIG, R_R1 + half)
@@ -350,11 +362,13 @@
                     mine[pl.ds(half * KB, KB)] = total
 
         give(0)
-        slots(1)
+        keep(0)
+        slots(2)
         give(1)
-        keep(0)
-        slots(1)
+        add_pair(0)
+        slots(2)
         keep(1)
+        add_pair(1)
 
         def match_hidden(j):
             for k in range(4):
@@ -402,28 +416,23 @@
 
         until(T_R1[0])
         sum_first(0)
+        until(T_R1[1])
+        sum_first(1)
         until(T_H2)
         arrived(qhv.at[0:48], R_H2)
         for s in (1, 2, 3):
             share_rows(qhv, s, sibling, S_H2, R_H3)
-        until(T_R1[1])
-        sum_first(1)
+        for half in (0, 1):
+            until(T_R2[half])
+            sum_second(half)
+        for half in (0, 1):
+            until(T_P1[half])
+            gather_first(half)
         until(T_H3)
         load_hid.wait()
         arrived(qhv.at[0:64], R_H3)
         hm[...] = jnp.zeros_like(hm)
-        slots(2, match_hidden)
-        until(T_R2[0])
-        sum_second(0)
-        slots(2, lambda j: match_hidden(j + 2))
-        until(T_R2[1])
-        sum_second(1)
-        slots(2, lambda j: match_hidden(j + 4))
-        until(T_P1[0])
-        gather_first(0)
-        slots(1, lambda j: match_hidden(j + 6))
-        until(T_P1[1])
-        gather_first(1)
+        slots(F // 2048, match_hidden)
 
         gm[...] = jnp.zeros_like(gm)
         GROUP = KB // W
@@ -439,50 +448,50 @@
         def done_at(first):
             t = lax.rem(first + NZ * depth, NCH)
             other = NZ * (LAYERS - 1 - t // NZ) + lax.rem(t, NZ)
-            return jnp.where(t < NZ * depth, jnp.maximum(t, other), t) + GROUP - 1
-
-        cutoff = T_P2[0]
+            return 2 * (jnp.where(t < NZ * depth, jnp.maximum(t, other), t) + GROUP - 1) + 1
+
+        late = []
 
         def early(own_side, half):
-            def one(j):
-                first = first_chunk(own_side, j, half)
-
-                @pl.when(done_at(first) < cutoff)
-                def _():
-                    match_group(first)
-
-            if CHAIN and now[0] < NCH:
-                slots(4, one)
-            else:
+            seen = now[0]
+            if not CHAIN or seen >= SLOTS:
                 for j in range(4):
                     match_group(first_chunk(own_side, j, half))
+                return
+
+            def two(j):
+                for k in (0, 1):
+                    first = first_chunk(own_side, 2 * j + k, half)
+
+                    @pl.when(done_at(first) < seen)
+                    def _(first=first):
+                        match_group(first)
+
+            slots(2, two)
+            late.append((own_side, half, seen))
 
         until(T_P2[0])
-        late = []
-        for half in (0, 1):
-            until(T_P2[half])
-            gather_second(half)
-            if half == 1:
-                until(NCH)
-            if now[0] < NCH and CHAIN:
-                late.append((True, half))
-            early(True, half)
-            arrived(prec.at[0:2048], R_P3 + half)
-            if now[0] < NCH and CHAIN:
-                late.append((False, half))
-            early(False, half)
-        until(NCH)
-        for own_side, half in late:
+        gather_second(0)
+        early(True, 0)
+        until(T_P2[1])
+        gather_second(1)
+        arrived(prec.at[0:2048], R_P3)
+        early(False, 0)
+        until(SLOTS)
+        early(True, 1)
+        arrived(prec.at[0:2048], R_P3 + 1)
+        early(False, 1)
+        for own_side, half, seen in late:
             for j in range(4):
                 first = first_chunk(own_side, j, half)
 
-                @pl.when(done_at(first) >= cutoff)
+                @pl.when(done_at(first) >= seen)
                 def _(first=first):
                     match_group(first)
     else:
         load_bas.wait()
         load_hid.wait()
-        until(NCH)
+        until(SLOTS)
 
     if COL:
         prod = gm[...] * hm[...]
@@ -584,7 +593,7 @@
             pltpu.VMEM((7, 8, 128), f32),
             pltpu.VMEM((4096, 128), bf16),
             pltpu.VMEM((4096, 128), bf16),
-            pltpu.VMEM((2048, 128), f32),
+            pltpu.VMEM((4096, 128), f32),
             pltpu.VMEM((1024, 128), f32),
             pltpu.VMEM((4096, 128), bf16),
             pltpu.VMEM((3, 1024, 128), bf16),
@@ -601,7 +610,7 @@
             dma,
             dma((NCH - NZ,)),
             dma,
-            dma((NUP // 2,)),
+            dma((NUP,)),
             dma((N_S,)),
             dma((N_R,)),
             dma,

time: 65.3 us -> 63 us (0.965)
  Pallas kernels: 64.6 us -> 62.3 us
    pallas_call x1, Pallas kernels: 63.2 us -> 60.9 us  [column(): pl.pallas_call(kernel, out_shape=(pltpu.VMEM((1, 128, D), bf16), pltpu.VM...]
where the time goes in v5:
time: 63 us; the launch traced here: 62.9 us
  Pallas kernels  62.3 us (99%)
  between operations  0.64 us (1%)
    pallas_call x1, Pallas kernels, column(): pl.pallas_call(kernel, out_shape=(pltpu.VMEM((1, 128, D), bf16), pltpu.VM...  60.9 us
    pallas_call x1, Pallas kernels, column(): pl.pallas_call(store, out_shape=(jax.ShapeDtypeStruct((1, 128, D), bf16),...  1.36 us

profile of v5, /device:TPU:1, one launch (start us, length us, event | category | flops | bytes accessed | tf_op | source)
XLA Modules:
  0.0 62.9 jit_solution(5760932626778578007)
XLA Ops:
  0.6 60.9 %shard_map.77 = (bf16[1,128,8192]{2,1,0:T(8,128)(2,1)S(1)}, f32[2,8]{1,0:T(2,128)S(1)}) custom-call(bf16[1,128,8192]{2,1,0:T(8,128)(2,1)} %inc.1, bf16[1,128,14336]{2,1,0:T(8,128)(2,1)} %hid.1, f32[1,8192,128]{2,1,0:T(8,128)} %bas.1, f32[1,128]{1,0:T(1,128)} %eig.1, bf16[1,4,8192]{2,1,0:T(4,128)(2,1)} %qg.1, bf16[1,4,14336]{2,1,0:T(4,128)(2,1)} %qh.1), custom_call_target="tpu_custom_call" | custom-call | tf_op jit(solution)/shard_map/pallas_call | solution.py:565
  61.6 1.4 %shard_map.78 = (bf16[1,128,8192]{2,1,0:T(8,128)(2,1)}, f32[2,8]{1,0:T(2,128)}) custom-call(bf16[1,128,8192]{2,1,0:T(8,128)(2,1)S(1)} %get-tuple-element.4.section, f32[2,8]{1,0:T(2,128)S(1)} %get-tuple-element.5.scores), custom_call_target="tpu_custom_call" | custom-call | tf_op jit(solution)/shard_map/pallas_call | solution.py:624

commit v6 on v5

--- a/solution.py
+++ b/solution.py
@@ -21,13 +21,13 @@
 R_E1, R_E2, R_E3, R_G1, R_H1, R_H2, R_H3 = range(7)
 R_G2, R_G3, R_PAIR, R_R1, R_R2, R_P1, R_P2, R_P3, N_R = range(7, 25, 2)
 SLOTS = 2 * NCH
-T_H1S, T_G1, T_H1, T_H2, T_H3 = 8, 10, 18, 43, 51
+T_H1S, T_G1, T_H1, T_H2, T_H3 = 8, 10, 18, 43, 54
 T_G2 = (17, 21)
 T_G3 = (19, 23)
 T_R1 = (38, 42)
-T_R2 = (45, 48)
-T_P1 = (49, 51)
-T_P2 = (57, 60)
+T_R2 = (45, 49)
+T_P1 = (51, 54)
+T_P2 = (59, 62)
 PER_P = 8
 KB = 512
 HALF = D // 2
@@ -84,7 +84,7 @@
 
     barrier = pltpu.get_barrier_semaphore()
     greeted = [sibling] + [on1(s) for s in (1, 2, 3)] + [on2(s) for s in (1, 2, 3)]
-    greeted += [onz(s) for s in range(1, LAYERS)]
+    greeted += [onz(1), onz(LAYERS - 1)]
     for dev in greeted:
         pl.semaphore_signal(barrier, inc=1, device_id=dev, device_id_type=MESH)
 
@@ -98,17 +98,17 @@
     ]
     for copy in small + [load_own, load_bas, load_hid]:
         copy.start()
-    for copy in small:
-        copy.wait()
 
     def fold(q, wide):
         rows = q[0].astype(f32)
         return jnp.concatenate([rows[:, s * wide:(s + 1) * wide] for s in range(4)], axis=0).astype(bf16)
 
+    pl.semaphore_wait(barrier, len(greeted))
+    for copy in small:
+        copy.wait()
     g16[...] = fold(qgr, D // 4)
     h16[...] = fold(qhr, F // 4)
     ebs[0] = jnp.broadcast_to(eigv[...], (8, 128))
-    pl.semaphore_wait(barrier, len(greeted))
 
     def post(src, dst, dev, send, recv):
         copy = remote(src, dst, cs.at[send], cr.at[recv], dev)
@@ -328,16 +328,11 @@
         project(1)
         damping = DAMP * jnp.sum(ebs[3][0:1], axis=1, keepdims=True) / K
         weighted = (accp[:, :128] + accp[:, 128:]) / (eigv[...] + damping)
-        hi, lo = split(weighted.T)
-        wmat[0:128, 0:128] = hi
-        wmat[128:256, 0:128] = hi
-        wmat[0:128, 128:256] = lo
-        wmat[128:256, 128:256] = jnp.zeros_like(lo)
+        wmat[...] = weighted.T.astype(bf16)
 
         def expand(side, half):
             at = pl.ds(pl.multiple_of(side * 4096 + half * 2048, 2048), 2048)
-            both = jnp.dot(bhl[at], wmat[...], preferred_element_type=f32)
-            return both[:, :128] + both[:, 128:]
+            return jnp.dot(bhl[at, 0:128], wmat[...], preferred_element_type=f32)
 
         def block_rows(block, half):
             return pl.ds(pl.multiple_of(half * 2048 + block * KB, KB), KB)
@@ -362,12 +357,14 @@
                     mine[pl.ds(half * KB, KB)] = total
 
         give(0)
+        slots(1)
+        give(1)
         keep(0)
-        slots(2)
-        give(1)
+        slots(1)
+        keep(1)
+        slots(1)
         add_pair(0)
-        slots(2)
-        keep(1)
+        slots(1)
         add_pair(1)
 
         def match_hidden(j):
@@ -600,7 +597,7 @@
             pltpu.VMEM((1024, 128), bf16),
             pltpu.VMEM((3, 256, 128), bf16),
             pltpu.VMEM((D, 128), bf16),
-            pltpu.VMEM((256, 256), bf16),
+            pltpu.VMEM((128, 128), bf16),
             pltpu.VMEM((128, 256), f32),
             pltpu.VMEM((128, 128), f32),
             pltpu.VMEM((128, 128), f32),

time: 63 us -> 61.6 us (0.978)
  Pallas kernels: 62.3 us -> 60.8 us
    pallas_call x1, Pallas kernels: 60.9 us -> 59.5 us  [column(): pl.pallas_call(kernel, out_shape=(pltpu.VMEM((1, 128, D), bf16), pltpu.VM...]
where the time goes in v6:
time: 61.6 us; the launch traced here: 61.5 us
  Pallas kernels  60.8 us (99%)
  between operations  0.64 us (1%)
    pallas_call x1, Pallas kernels, column(): pl.pallas_call(kernel, out_shape=(pltpu.VMEM((1, 128, D), bf16), pltpu.VM...  59.5 us
    pallas_call x1, Pallas kernels, column(): pl.pallas_call(store, out_shape=(jax.ShapeDtypeStruct((1, 128, D), bf16),...  1.36 us

profile of v6, /device:TPU:1, one launch (start us, length us, event | category | flops | bytes accessed | tf_op | source)
XLA Modules:
  0.0 61.5 jit_solution(7678867551800243919)
XLA Ops:
  0.6 59.5 %shard_map.77 = (bf16[1,128,8192]{2,1,0:T(8,128)(2,1)S(1)}, f32[2,8]{1,0:T(2,128)S(1)}) custom-call(bf16[1,128,8192]{2,1,0:T(8,128)(2,1)} %inc.1, bf16[1,128,14336]{2,1,0:T(8,128)(2,1)} %hid.1, f32[1,8192,128]{2,1,0:T(8,128)} %bas.1, f32[1,128]{1,0:T(1,128)} %eig.1, bf16[1,4,8192]{2,1,0:T(4,128)(2,1)} %qg.1, bf16[1,4,14336]{2,1,0:T(4,128)(2,1)} %qh.1), custom_call_target="tpu_custom_call" | custom-call | tf_op jit(solution)/shard_map/pallas_call | solution.py:562
  60.1 1.4 %shard_map.78 = (bf16[1,128,8192]{2,1,0:T(8,128)(2,1)}, f32[2,8]{1,0:T(2,128)}) custom-call(bf16[1,128,8192]{2,1,0:T(8,128)(2,1)S(1)} %get-tuple-element.4.section, f32[2,8]{1,0:T(2,128)S(1)} %get-tuple-element.5.scores), custom_call_target="tpu_custom_call" | custom-call | tf_op jit(solution)/shard_map/pallas_call | solution.py:621

commit v7 on v6

--- a/solution.py
+++ b/solution.py
@@ -21,16 +21,17 @@
 R_E1, R_E2, R_E3, R_G1, R_H1, R_H2, R_H3 = range(7)
 R_G2, R_G3, R_PAIR, R_R1, R_R2, R_P1, R_P2, R_P3, N_R = range(7, 25, 2)
 SLOTS = 2 * NCH
-T_H1S, T_G1, T_H1, T_H2, T_H3 = 8, 10, 18, 43, 54
+T_H1S, T_G1, T_H1, T_H2, T_H3 = 8, 8, 18, 43, 54
 T_G2 = (17, 21)
 T_G3 = (19, 23)
 T_R1 = (38, 42)
 T_R2 = (45, 49)
 T_P1 = (51, 54)
-T_P2 = (59, 62)
+T_P2 = (57, 60)
 PER_P = 8
 KB = 512
 HALF = D // 2
+AHEAD = 14
 STORES = 4
 CHAIN = True
 COL = True
@@ -118,7 +119,7 @@
         remote(like, like, cs.at[0], cr.at[recv], sibling).wait_recv()
 
     def link(i, t):
-        return remote(down.at[i], rcv.at[i], chain_s, chain_r.at[t], onz(LAYERS - 1))
+        return remote(down.at[i], rcv.at[i], chain_s, chain_r.at[lax.rem(t, AHEAD)], onz(LAYERS - 1))
 
     def uplink(n):
         return remote(ups.at[n], upr.at[n], up_s, up_r.at[n], onz(1))
@@ -476,8 +477,6 @@
         early(False, 0)
         until(SLOTS)
         early(True, 1)
-        arrived(prec.at[0:2048], R_P3 + 1)
-        early(False, 1)
         for own_side, half, seen in late:
             for j in range(4):
                 first = first_chunk(own_side, j, half)
@@ -485,6 +484,9 @@
                 @pl.when(done_at(first) >= seen)
                 def _(first=first):
                     match_group(first)
+
+        arrived(prec.at[0:2048], R_P3 + 1)
+        early(False, 1)
     else:
         load_bas.wait()
         load_hid.wait()
@@ -605,7 +607,7 @@
             dma((6,)),
             dma,
             dma,
-            dma((NCH - NZ,)),
+            dma((AHEAD,)),
             dma,
             dma((NUP,)),
             dma((N_S,)),

time: 61.6 us -> 60.9 us (0.989)
    pallas_call x1, Pallas kernels: 59.5 us -> 58.8 us  [column(): pl.pallas_call(kernel, out_shape=(pltpu.VMEM((1, 128, D), bf16), pltpu.VM...]
where the time goes in v7:
time: 60.9 us; the launch traced here: 60.8 us
  Pallas kernels  60.2 us (99%)
  between operations  0.64 us (1%)
    pallas_call x1, Pallas kernels, column(): pl.pallas_call(kernel, out_shape=(pltpu.VMEM((1, 128, D), bf16), pltpu.VM...  58.8 us
    pallas_call x1, Pallas kernels, column(): pl.pallas_call(store, out_shape=(jax.ShapeDtypeStruct((1, 128, D), bf16),...  1.36 us

profile of v7, /device:TPU:1, one launch (start us, length us, event | category | flops | bytes accessed | tf_op | source)
XLA Modules:
  0.0 60.8 jit_solution(3833380196669984849)
XLA Ops:
  0.6 58.8 %shard_map.77 = (bf16[1,128,8192]{2,1,0:T(8,128)(2,1)S(1)}, f32[2,8]{1,0:T(2,128)S(1)}) custom-call(bf16[1,128,8192]{2,1,0:T(8,128)(2,1)} %inc.1, bf16[1,128,14336]{2,1,0:T(8,128)(2,1)} %hid.1, f32[1,8192,128]{2,1,0:T(8,128)} %bas.1, f32[1,128]{1,0:T(1,128)} %eig.1, bf16[1,4,8192]{2,1,0:T(4,128)(2,1)} %qg.1, bf16[1,4,14336]{2,1,0:T(4,128)(2,1)} %qh.1), custom_call_target="tpu_custom_call" | custom-call | tf_op jit(solution)/shard_map/pallas_call | solution.py:564
  59.5 1.4 %shard_map.78 = (bf16[1,128,8192]{2,1,0:T(8,128)(2,1)}, f32[2,8]{1,0:T(2,128)}) custom-call(bf16[1,128,8192]{2,1,0:T(8,128)(2,1)S(1)} %get-tuple-element.4.section, f32[2,8]{1,0:T(2,128)S(1)} %get-tuple-element.5.scores), custom_call_target="tpu_custom_call" | custom-call | tf_op jit(solution)/shard_map/pallas_call | solution.py:623

commit v8 on v7

--- a/solution.py
+++ b/solution.py
@@ -19,9 +19,10 @@
 NUP = NZ * (LAYERS - 1)
 S_E, S_G1, S_H1, S_G2, S_H2, S_BIG, S_SMALL, N_S = range(8)
 R_E1, R_E2, R_E3, R_G1, R_H1, R_H2, R_H3 = range(7)
-R_G2, R_G3, R_PAIR, R_R1, R_R2, R_P1, R_P2, R_P3, N_R = range(7, 25, 2)
+R_G2, R_G3, R_PAIR, R_R1, R_R2, R_P1, R_P3, R_P2 = range(7, 23, 2)
+N_R = R_P2 + 6
 SLOTS = 2 * NCH
-T_H1S, T_G1, T_H1, T_H2, T_H3 = 8, 8, 18, 43, 54
+T_H1S, T_G1, T_H1, T_H2, T_H3 = 8, 8, 16, 43, 53
 T_G2 = (17, 21)
 T_G3 = (19, 23)
 T_R1 = (38, 42)
@@ -32,7 +33,7 @@
 KB = 512
 HALF = D // 2
 AHEAD = 14
-STORES = 4
+STORES = 1
 CHAIN = True
 COL = True
 
@@ -58,7 +59,7 @@
     own, down, rcv, ups, upr, fin, hidv, basv, bhl, eigv, qgr, qhr,
     g16, h16, a1g, a1h, qgv, qhv, ebs, ebr,
     part_out, part_in, kept, mine, r1s, r1r, r2s, r2r, prec,
-    wmat, accp, gm, hm, share,
+    wmat, accp, gm, hm, pick, share,
     ld_sem, out_sem, chain_s, chain_r, up_s, up_r, cs, cr, zs, zr,
 ):
     z = lax.axis_index("segment")
@@ -403,12 +404,12 @@
             arrived(prec.at[0:384], R_P1 + half)
             rows = band(0, half)
             for s in (2, 1, 3):
-                post(prec.at[rows], prec.at[rows], on1(s), S_BIG, R_P2 + half)
+                post(prec.at[rows], prec.at[rows], on1(s), S_BIG, R_P2 + 3 * half + s - 1)
             post(prec.at[rows], prec.at[rows], sibling, S_BIG, R_P3 + half)
 
         def gather_second(half):
-            arrived(prec.at[0:3 * KB], R_P2 + half)
-            for s in (1, 2, 3):
+            for s in (1, 3, 2):
+                arrived(prec.at[0:KB], R_P2 + 3 * half + s - 1)
                 rows = band(s, half)
                 post(prec.at[rows], prec.at[rows], sibling, S_BIG, R_P3 + half)
 
@@ -429,6 +430,12 @@
         until(T_H3)
         load_hid.wait()
         arrived(qhv.at[0:64], R_H3)
+        pos = lax.broadcasted_iota(jnp.int32, (128, 128), 0)
+        side = pos // 64
+        p2nd = (pos // 16) % 4
+        p1st = (pos // 4) % 4
+        query = jnp.where(side == 0, p2nd * 2 + p1st // 2, p1st * 2 + p2nd // 2)
+        pick[...] = (query == lax.broadcasted_iota(jnp.int32, (128, 128), 1)).astype(f32)
         hm[...] = jnp.zeros_like(hm)
         slots(F // 2048, match_hidden)
 
@@ -494,16 +501,10 @@
 
     if COL:
         prod = gm[...] * hm[...]
-        pos = lax.broadcasted_iota(jnp.int32, (128, 128), 0)
-        side = pos // 64
-        p2nd = (pos // 16) % 4
-        p1st = (pos // 4) % 4
-        query = jnp.where(side == 0, p2nd * 2 + p1st // 2, p1st * 2 + p2nd // 2)
-        pick = (query == lax.broadcasted_iota(jnp.int32, (128, 128), 1)).astype(f32)
         sums = [jnp.sum(prod[s * SEQLEN:(s + 1) * SEQLEN], axis=0, keepdims=True) for s in (0, 1)]
         line = lax.broadcasted_iota(jnp.int32, (8, 128), 0)
         both = jnp.where(line == 0, sums[0], jnp.where(line == 1, sums[1], 0.0))
-        tile = jnp.dot(both, pick, precision=lax.Precision.HIGHEST, preferred_element_type=f32)
+        tile = jnp.dot(both, pick[...], precision=lax.Precision.HIGHEST, preferred_element_type=f32)
         share[z] = tile / (SEQLEN * QLEN)
         for s in (4, 3, 5, 2, 6, 1, 7):
             remote(share.at[z], share.at[z], zs, zr, onz(s)).start()
@@ -603,6 +604,7 @@
             pltpu.VMEM((128, 256), f32),
             pltpu.VMEM((128, 128), f32),
             pltpu.VMEM((128, 128), f32),
+            pltpu.VMEM((128, 128), f32),
             pltpu.VMEM((LAYERS, 8, 128), f32),
             dma((6,)),
             dma,

time: 60.9 us -> 60.9 us (level)
  no operation moved by 1% of the time
where the time goes in v8:
time: 60.9 us
  Pallas kernels  60.2 us (99%)
  between operations  0.64 us (1%)
    pallas_call x1, Pallas kernels, column(): pl.pallas_call(kernel, out_shape=(pltpu.VMEM((1, 128, D), bf16), pltpu.VM...  58.9 us
    pallas_call x1, Pallas kernels, column(): pl.pallas_call(store, out_shape=(jax.ShapeDtypeStruct((1, 128, D), bf16),...  1.34 us

profile of v8, /device:TPU:1, one launch (start us, length us, event | category | flops | bytes accessed | tf_op | source)
XLA Modules:
  0.0 60.9 jit_solution(1696317354061956044)
XLA Ops:
  0.6 58.9 %shard_map.77 = (bf16[1,128,8192]{2,1,0:T(8,128)(2,1)S(1)}, f32[2,8]{1,0:T(2,128)S(1)}) custom-call(bf16[1,128,8192]{2,1,0:T(8,128)(2,1)} %inc.1, bf16[1,128,14336]{2,1,0:T(8,128)(2,1)} %hid.1, f32[1,8192,128]{2,1,0:T(8,128)} %bas.1, f32[1,128]{1,0:T(1,128)} %eig.1, bf16[1,4,8192]{2,1,0:T(4,128)(2,1)} %qg.1, bf16[1,4,14336]{2,1,0:T(4,128)(2,1)} %qh.1), custom_call_target="tpu_custom_call" | custom-call | tf_op jit(solution)/shard_map/pallas_call | solution.py:565
  59.5 1.3 %shard_map.78 = (bf16[1,128,8192]{2,1,0:T(8,128)(2,1)}, f32[2,8]{1,0:T(2,128)}) custom-call(bf16[1,128,8192]{2,1,0:T(8,128)(2,1)S(1)} %get-tuple-element.4.section, f32[2,8]{1,0:T(2,128)S(1)} %get-tuple-element.5.scores), custom_call_target="tpu_custom_call" | custom-call | tf_op jit(solution)/shard_map/pallas_call | solution.py:625
